TPU v7x, 32 devices: a whole 2x2x4 slice. The times are simulated.
32 devices in a mesh: dp: 8 (over z, y), mp: 4 (over x, core).
Axes of the slice: x: 2, y: 2, z: 4, core: 2. Of those that a mesh axis runs over, the one named last changes fastest.
Arguments:
- hidden: bfloat16 [128, 5120], P('dp', 'mp'), may hold values from -6 to 6
- w_query: bfloat16 [5120, 8192], P(None, 'mp'), may hold values from -0.078125 to 0.078125
- w_key: bfloat16 [5120, 1024], P(None, 'mp'), may hold values from -0.078125 to 0.078125
- w_value: bfloat16 [5120, 1024], P(None, 'mp'), may hold values from -0.078125 to 0.078125
- query_gain: float32 [128], replicated, may hold values from 0.5 to 3
- key_gain: float32 [128], replicated, may hold values from 0.5 to 3
- kv_pool: bfloat16 [6144, 16, 8, 256], P('dp', None, 'mp')
- page_table: int32 [128, 48], replicated, may hold values from 0 to 767, as said below
- parent: int32 [128], replicated, may hold values from 0 to 127, as said below
- surviving: int32 [128], replicated, may hold values from 0 to 1, as said below
Outputs:
- refilled_pool: bfloat16 [6144, 16, 8, 256], P('dp', None, 'mp')
- attention: bfloat16 [128, 8192], P('dp', 'mp')
Inputs may be any that keep to these rules, and one draw needn't show every extreme that they name: `page_table`: for each group, its 16 rows together name each page 0 to 767 once. A pruned branch's parent survives. For every group, at most 2 of its pruned branches have parents in any one group, and this is reached in every draw; those branches have different parents. For a surviving branch the entry names some surviving branch and is not used. `surviving`: each group keeps 2 to 4 of its branches.
All inputs are finite; a program needn't handle non-finite values.
Results may differ from a plain program's by a relative error of at most 0.015.
The roundings to bfloat16 on the way count: a program that leaves them out, or rounds other values in their place, can miss the bound.
Values may be sent and summed in bfloat16 or wider, within the bound.
No kernel may reach another device: no remote copies, remote signals or barrier semaphores. Data moves between devices by JAX's collectives and lax.ppermute only.
A program may use at most 192 MiB of HBM per device.

v0:
```python
import functools
import math

import jax
import jax.numpy as jnp
from jax import lax
from jax.experimental import pallas as pl
from jax.experimental.pallas import tpu as pltpu
from jax.sharding import PartitionSpec as P

H = 64
KVH = 8
HD = 128
PAGE = 16
NPAGE = 48
CAP = 2
KEEP = 4
NZ = 4
ROUNDS = 40
LANES = 128
PREFIX = 8
FIRST = 2
REST = 2
PIECES = 2
ROOM = 48 * 1024 * 1024
NEVER = 1 << 20


def normalize(values, gain):
    return values * lax.rsqrt(jnp.mean(values * values, -1, keepdims=True) + 1e-06) * gain


def plan_kernel(groups, branch_count, parent_row, alive_row, parent_column, alive_column, out, state):
    ny = groups // NZ
    branches = groups * branch_count
    shifts = list(range(1, ny))
    slots = NZ * KEEP
    me = lax.axis_index("dp")

    def iota(shape, axis):
        return lax.broadcasted_iota(jnp.int32, shape, axis)

    square = (branches, branches)
    down_ids, across_ids = iota(square, 0), iota(square, 1)
    same = lax.div(down_ids, branch_count) == lax.div(across_ids, branch_count)
    alive_r, alive_c = alive_row[...] > 0, alive_column[...] > 0
    before = jnp.where(same & (down_ids < across_ids) & alive_c, 1, 0)
    item_row = jnp.sum(before, axis=0, keepdims=True)
    item_row = item_row + lax.div(iota((1, branches), 1), branch_count) * KEEP
    before = jnp.where(same & (across_ids < down_ids) & alive_r, 1, 0)
    item_column = jnp.sum(before, axis=1, keepdims=True)
    item_column = item_column + lax.div(iota((branches, 1), 0), branch_count) * KEEP
    wanted = jnp.sum(
        jnp.where(parent_column[...] == across_ids, item_row, 0), axis=1, keepdims=True
    )
    wanted = jnp.where(alive_c, -1, wanted)
    wide = (branches, LANES)
    local = lax.rem(iota(wide, 0), branch_count)
    takes = jnp.where(wanted == iota(wide, 1), local, -1)
    child = jnp.max(takes.reshape(groups, branch_count, LANES), axis=1)
    holds = jnp.where((item_column == iota(wide, 1)) & alive_c, local, -1)
    branch = jnp.max(holds, axis=0, keepdims=True)

    shape = (groups, LANES)
    here, item = iota(shape, 0), iota(shape, 1)
    z, y = lax.div(here, ny), lax.rem(here, ny)
    source = lax.div(item, KEEP)
    item_z, item_y = lax.div(source, ny), lax.rem(source, ny)
    on_line = item_y == y
    need = child >= 0

    def across(mask):
        return jnp.max(jnp.where(mask, 1, 0), axis=0, keepdims=True)

    top = jnp.max(jnp.where(need, z, -1), axis=0, keepdims=True)
    bottom = jnp.min(jnp.where(need, z, NZ), axis=0, keepdims=True)
    top_crosses = across(need & (z == top) & (item_y != y))
    bottom_crosses = across(need & (z == bottom) & (item_y != y))
    tie = LANES - 1 - item
    up_hops, down_hops = jnp.maximum(top - z, 0), jnp.maximum(z - bottom, 0)
    up_key = (up_hops * 2 + top_crosses) * LANES + tie
    down_key = (down_hops * 2 + bottom_crosses) * LANES + tie
    go_up, go_down = on_line & (up_hops > 0), on_line & (down_hops > 0)

    def beside(x, shift):
        return jnp.where(
            y + shift < ny, pltpu.roll(x, groups - shift, 0), pltpu.roll(x, (ny - shift) % groups, 0)
        )

    crosses = [on_line & (beside(child, shift) >= 0) for shift in shifts]
    own = source == here
    start = [go_up & own, go_down & own] + [c & own for c in crosses]
    rows = len(start)
    for i, mask in enumerate(start):
        state[i] = jnp.where(mask, 0, NEVER)
        state[rows + i] = jnp.full(shape, -1, jnp.int32)

    def choose(i, r, key):
        ready = state[i]
        key = jnp.where(ready <= r, key(ready), -1)
        best = jnp.max(key, axis=1, keepdims=True)
        chosen = (key == best) & (best >= 0)
        state[i] = jnp.where(chosen, NEVER, ready)
        state[rows + i] = jnp.where(chosen, r, state[rows + i])
        return jnp.where(chosen, 1, 0)

    def one_round(r):
        ups = choose(0, r, lambda ready: up_key)
        downs = choose(1, r, lambda ready: down_key)
        for i in range(2, rows):
            choose(i, r, lambda ready: (ROUNDS - ready) * LANES + tie)
        ups = jnp.where(z > 0, pltpu.roll(ups, ny, 0), 0) > 0
        downs = jnp.where(z < NZ - 1, pltpu.roll(downs, groups - ny, 0), 0) > 0
        rested = jnp.where(r < FIRST, FIRST, r + REST)
        state[0] = jnp.where(ups & go_up, rested, state[0])
        state[1] = jnp.where(downs & go_down, rested, state[1])
        left = jnp.minimum(state[0], state[1])
        for i, cross in enumerate(crosses):
            there = jnp.where((ups | downs) & cross, jnp.maximum(r + 1, FIRST), state[2 + i])
            state[2 + i] = there
            left = jnp.minimum(left, there)
        return r + 1, jnp.min(left)

    rounds, _ = lax.while_loop(
        lambda carry: (carry[1] < NEVER) & (carry[0] < ROUNDS),
        lambda carry: one_round(carry[0]),
        (jnp.int32(0), jnp.int32(0)),
    )

    def row_of(x, group):
        return jnp.max(jnp.where(here == group, x, -1), axis=0, keepdims=True)

    my_z = lax.div(me, ny)
    my_y = me - my_z * ny
    even = lax.rem(my_z, 2) == 0
    item = iota((1, LANES), 1)
    group = lax.div(item, KEEP)
    slot = lax.div(group, ny) * KEEP + lax.rem(item, KEEP)
    value = jnp.where(group == me, slots + branch, slot)
    taker = row_of(child, me)
    up_out, down_out = row_of(state[rows], me), row_of(state[rows + 1], me)
    up_in, down_in = row_of(state[rows], me - ny), row_of(state[rows + 1], me + ny)
    outs = [jnp.where(even, up_out, down_out), jnp.where(even, down_out, up_out)]
    ins = [jnp.where(even, down_in, up_in), jnp.where(even, up_in, down_in)]
    for shift in shifts:
        outs.append(row_of(state[rows + 1 + shift], me))
        from_y = lax.rem(my_y + ny - shift, ny)
        ins.append(row_of(state[rows + 1 + shift], my_z * ny + from_y))
    table = [(times, value) for times in outs]
    table += [(times, slot) for times in ins[:2]]
    table += [(times, taker) for times in ins]
    at = iota((ROUNDS, LANES), 0)
    lane = iota((ROUNDS, LANES), 1)
    result = jnp.full((ROUNDS, LANES), -1, jnp.int32)
    for c, (times, values) in enumerate(table):
        column = jnp.max(jnp.where(times == at, values, -1), axis=1, keepdims=True)
        result = jnp.where(lane == c, column, result)
    out[pl.ds(0, ROUNDS), :] = result
    extra = iota((8, LANES), 0)
    out[pl.ds(ROUNDS, 8), :] = jnp.where(
        extra == 0, rounds, jnp.where(extra == 1, branch, jnp.where(extra == 2, taker, 0))
    )


class Plan:
    def __init__(self, links, groups, branch_count):
        self.links = links
        self.width = 2 * links + 2
        self.rounds_at = ROUNDS * self.width
        self.branch_at = self.rounds_at + 1
        self.taker_at = self.branch_at + groups * KEEP
        self.pages_at = self.taker_at + groups * KEEP

    def send(self, table, r, l):
        return table[r * self.width + l]

    def save(self, table, r, l):
        return table[r * self.width + self.links + l]

    def taker(self, table, r, l):
        return table[r * self.width + self.links + 2 + l]

    def page(self, table, branch, p):
        return table[self.pages_at + branch * NPAGE + p]

    def kept(self, table, k):
        return table[self.branch_at + lax.axis_index("dp") * KEEP + k]

    def own_taker(self, table, k):
        return table[self.taker_at + lax.axis_index("dp") * KEEP + k]


def routing(parent, surviving, page_table, groups, branch_count, links):
    ny = groups // NZ
    rows = 2 + ny - 1
    out = pl.pallas_call(
        functools.partial(plan_kernel, groups, branch_count),
        out_shape=jax.ShapeDtypeStruct((ROUNDS + 8, LANES), jnp.int32),
        in_specs=[VMEM] * 4,
        out_specs=VMEM,
        scratch_shapes=[pltpu.VMEM((2 * rows, groups, LANES), jnp.int32)],
        compiler_params=pltpu.CompilerParams(vmem_limit_bytes=ROOM),
        cost_estimate=pl.CostEstimate(flops=0, bytes_accessed=6_000_000, transcendentals=0),
        name="plan",
    )(
        parent.reshape(1, -1),
        surviving.reshape(1, -1),
        parent.reshape(-1, 1),
        surviving.reshape(-1, 1),
    )
    pages = lax.dynamic_slice_in_dim(
        page_table, lax.axis_index("dp") * branch_count, branch_count, 0
    )
    items = groups * KEEP
    return jnp.concatenate(
        [
            out[:ROUNDS, : 2 * links + 2].reshape(-1),
            out[ROUNDS, :1],
            out[ROUNDS + 1, :items],
            out[ROUNDS + 2, :items],
            pages.reshape(-1),
        ]
    )


SMEM = pl.BlockSpec(memory_space=pltpu.SMEM)
VMEM = pl.BlockSpec(memory_space=pltpu.VMEM)
HBM = pl.BlockSpec(memory_space=pltpu.HBM)
ANY = pl.BlockSpec(memory_space=pl.ANY)


def first_kernel(groups, branch_count, facts, pool, *refs):
    ny = groups // NZ
    packed, table, load_sem, sem = refs[:-3], refs[-3], refs[-2], refs[-1]
    load = pltpu.make_async_copy(facts, table, load_sem)
    load.start()
    me = lax.axis_index("dp")
    z, y = me // ny, me % ny
    shape = (branch_count, groups * branch_count)
    child = lax.broadcasted_iota(jnp.int32, shape, 1)
    local = lax.broadcasted_iota(jnp.int32, shape, 0)
    column = lax.broadcasted_iota(jnp.int32, (branch_count, 1), 0)
    parent, surviving = facts[pl.ds(NPAGE, 1), :], facts[pl.ds(NPAGE + 1, 1), :]
    mine = (surviving == 0) & (parent == me * branch_count + local)
    target = lax.div(child, branch_count)
    target_z = lax.div(target, ny)
    target_y = target - target_z * ny

    def seen(mask):
        return jnp.max(mask.astype(jnp.int32), axis=1, keepdims=True)

    def leading(key):
        rows = []
        for _ in range(FIRST):
            best = jnp.max(key)
            rows.append(
                jnp.where(best >= 0, branch_count - 1 - lax.rem(best, branch_count), -1)
            )
            key = jnp.where(key == best, -1, key)
        return rows

    ways = []
    for steps in (target_z - z, z - target_z):
        hops = jnp.max(jnp.where(mine, steps, 0), axis=1, keepdims=True)
        far_across = seen(mine & (steps == hops) & (target_y != y))
        key = (hops * 2 + far_across) * branch_count + branch_count - 1 - column
        ways.append(leading(jnp.where(hops > 0, key, -1)))
    even = lax.rem(z, 2) == 0
    sends = [
        [jnp.where(even, u, d) for u, d in zip(*ways)],
        [jnp.where(even, d, u) for u, d in zip(*ways)],
    ]
    for shift in range(1, ny):
        to = lax.rem(y + shift, ny)
        crossing = seen(mine & (target_z == z) & (target_y == to))
        sends.append(leading(jnp.where(crossing > 0, branch_count - 1 - column, -1)))
    load.wait()
    for l, rows in enumerate(sends):
        for r, row in enumerate(rows):

            @pl.when(row >= 0)
            def _():
                for p in range(NPAGE):
                    page = table[p, me * branch_count + row]
                    pltpu.make_async_copy(
                        pool.at[page], packed[l].at[r * NPAGE + p], sem.at[l, r]
                    ).start()

    for l, rows in enumerate(sends):
        for r, row in enumerate(rows):
            box = packed[l].at[pl.ds(r * NPAGE, NPAGE)]

            @pl.when(row >= 0)
            def _():
                pltpu.make_async_copy(box, box, sem.at[l, r]).wait()


def first_windows(groups, branch_count, facts, pool):
    links = 2 + groups // NZ - 1
    windows = jax.ShapeDtypeStruct((FIRST * NPAGE,) + pool.shape[1:], pool.dtype)
    return pl.pallas_call(
        functools.partial(first_kernel, groups, branch_count),
        out_shape=[windows] * links,
        in_specs=[VMEM, HBM],
        out_specs=[VMEM] * links,
        scratch_shapes=[
            pltpu.SMEM(facts.shape, facts.dtype),
            pltpu.SemaphoreType.DMA,
            pltpu.SemaphoreType.DMA((links, FIRST)),
        ],
        compiler_params=pltpu.CompilerParams(vmem_limit_bytes=ROOM),
        cost_estimate=pl.CostEstimate(flops=0, bytes_accessed=6_000_000, transcendentals=0),
        name="first_windows",
    )(facts, pool)


def step_kernel(plan, packs, files, traced, count, filing, attending, *refs):
    if traced:
        at, refs = refs[0][0], refs[1:]
        packs = [(at,) + entry[1:] for entry in packs]
        files = [(at,) + entry[1:] for entry in files]
    links = plan.links
    table = refs[0]
    arrived = refs[1 : 1 + count]
    pool, rows = refs[1 + count : 3 + count]
    store, refilled, out = refs[6 + count : 9 + count]
    packed = refs[9 + count : -8]
    row, result, row_sem, out_sem, file_sem, save_sem, pack_sem, fresh_sem = refs[-8:]
    slots = NZ * KEEP

    comes = []
    for r, l, first, pages, array, offset in files:
        part = arrived[array].at[pl.ds(offset, pages)]
        save = plan.save(table, r, l) if l < 2 else None
        comes.append((save, plan.taker(table, r, l), part, first, pages))

    def is_fresh(source):
        fresh = [source == save for save, _, _, _, _ in comes if save is not None]
        return (source >= 0) & functools.reduce(jnp.logical_or, fresh) if fresh else False

    goes = []
    for r, first, pages, which in packs:
        for l in which:
            goes.append((plan.send(table, r, l), packed[len(goes)], first, pages))

    for i, (source, box, first, pages) in enumerate(goes):

        @pl.when(source >= slots)
        def _():
            @pl.loop(0, pages, unroll=8)
            def _(p):
                page = plan.page(table, source - slots, first + p)
                pltpu.make_async_copy(pool.at[page], box.at[p], pack_sem.at[i]).start()

        @pl.when((source >= 0) & (source < slots) & jnp.logical_not(is_fresh(source)))
        def _():
            pltpu.make_async_copy(
                store.at[jnp.clip(source, 0, slots - 1), pl.ds(first, pages)],
                box,
                pack_sem.at[i],
            ).start()

        for save, _, part, file_first, file_pages in comes:
            if save is not None and file_first <= first < file_first + file_pages:

                @pl.when((source >= 0) & (source == save))
                def _():
                    pltpu.make_async_copy(
                        part.at[pl.ds(first - file_first, pages)], box, fresh_sem.at[i]
                    ).start()

    for i, (save, taker, part, first, pages) in enumerate(comes if filing else []):
        if save is not None:

            @pl.when(save >= 0)
            def _():
                pltpu.make_async_copy(
                    part, store.at[jnp.maximum(save, 0), pl.ds(first, pages)], save_sem.at[i]
                ).start()

        @pl.when(taker >= 0)
        def _():
            if attending:
                pltpu.make_async_copy(rows.at[taker], row.at[i], row_sem.at[i]).start()

            @pl.loop(0, pages, unroll=8)
            def _(p):
                page = plan.page(table, taker, first + p)
                pltpu.make_async_copy(part.at[p], refilled.at[page], file_sem.at[i]).start()

    if attending:
        attend_to(
            [taker for _, taker, _, _, _ in comes],
            [part for _, _, part, _, _ in comes],
            row,
            result,
            row_sem,
            out,
            out_sem,
        )

    for i, (source, box, first, pages) in enumerate(goes):

        @pl.when((source >= 0) & jnp.logical_not(is_fresh(source)))
        def _():
            pltpu.make_async_copy(box, box, pack_sem.at[i]).wait()

        if comes:

            @pl.when(is_fresh(source))
            def _():
                pltpu.make_async_copy(box, box, fresh_sem.at[i]).wait()

    for i, (save, taker, part, first, pages) in enumerate(comes if filing else []):
        if save is not None:

            @pl.when(save >= 0)
            def _():
                pltpu.make_async_copy(part, part, save_sem.at[i]).wait()

        @pl.when(taker >= 0)
        def _():
            pltpu.make_async_copy(part, part, file_sem.at[i]).wait()


def step(plan, packs, files, at, table, arrived, pool, rows, store, refilled, attention, filing=True, attending=False):
    at = [] if at is None else [jnp.stack([at])]
    count = len(arrived)
    lead = len(at) + 1 + count
    heads = rows.shape[2]
    boxes = [
        jax.ShapeDtypeStruct((pages,) + pool.shape[1:], pool.dtype)
        for _, _, pages, which in packs
        for _ in which
    ]
    some = max(len(files), 1)
    out = pl.pallas_call(
        functools.partial(step_kernel, plan, packs, files, bool(at), count, filing, attending),
        out_shape=[
            jax.ShapeDtypeStruct(array.shape, array.dtype) for array in (store, refilled, attention)
        ]
        + boxes,
        in_specs=[SMEM] * (len(at) + 1) + [VMEM] * count + [HBM, ANY, HBM, HBM, ANY],
        out_specs=[HBM] * 2 + [ANY] + [VMEM] * len(boxes),
        scratch_shapes=[
            pltpu.VMEM((some, 3, heads, HD), rows.dtype),
            pltpu.VMEM((some, heads, HD), attention.dtype),
        ]
        + [pltpu.SemaphoreType.DMA((some,))] * 4
        + [pltpu.SemaphoreType.DMA((max(len(boxes), 1),))] * 2,
        input_output_aliases={lead + 2: 0, lead + 3: 1, lead + 4: 2},
        compiler_params=pltpu.CompilerParams(vmem_limit_bytes=ROOM),
        cost_estimate=pl.CostEstimate(flops=0, bytes_accessed=6_000_000, transcendentals=0),
        name="step",
    )(*at, table, *arrived, pool, rows, store, refilled, attention)
    return out[0], out[1], out[2], list(out[3:])


def own_kernel(plan, table, pool, token, refilled, store, window, in_sem, out_sem):
    moves = [
        (plan.kept(table, k), [plan.kept(table, k), plan.own_taker(table, k)]) for k in range(KEEP)
    ]
    for k, (source, _) in enumerate(moves):

        @pl.when(source >= 0)
        def _():
            @pl.loop(0, NPAGE, unroll=8)
            def _(p):
                pltpu.make_async_copy(
                    pool.at[plan.page(table, source, p)], window.at[k, p], in_sem.at[k]
                ).start()

    for k, (source, targets) in enumerate(moves):

        @pl.when(source >= 0)
        def _():
            pltpu.make_async_copy(window.at[k], window.at[k], in_sem.at[k]).wait()

        for lane, to in enumerate(targets):

            @pl.when((source >= 0) & (to >= 0))
            def _():
                @pl.loop(0, NPAGE, unroll=8)
                def _(p):
                    pltpu.make_async_copy(
                        window.at[k, p], refilled.at[plan.page(table, to, p)], out_sem.at[k, lane]
                    ).start()

    for k, (source, targets) in enumerate(moves):
        for lane, to in enumerate(targets):

            @pl.when((source >= 0) & (to >= 0))
            def _():
                pltpu.make_async_copy(window.at[k], window.at[k], out_sem.at[k, lane]).wait()


def own_windows(plan, table, pool, token):
    return pl.pallas_call(
        functools.partial(own_kernel, plan),
        out_shape=[
            jax.ShapeDtypeStruct(pool.shape, pool.dtype),
            jax.ShapeDtypeStruct((NZ * KEEP, NPAGE) + pool.shape[1:], pool.dtype),
        ],
        in_specs=[SMEM, HBM, ANY],
        out_specs=[HBM] * 2,
        scratch_shapes=[
            pltpu.VMEM((KEEP, NPAGE) + pool.shape[1:], pool.dtype),
            pltpu.SemaphoreType.DMA((KEEP,)),
            pltpu.SemaphoreType.DMA((KEEP, 2)),
        ],
        compiler_params=pltpu.CompilerParams(vmem_limit_bytes=ROOM),
        cost_estimate=pl.CostEstimate(flops=0, bytes_accessed=9_000_000, transcendentals=0),
        name="own_windows",
    )(table, pool, token)


def attend_to(branch, windows, row, result, row_sem, out, out_sem):
    count = len(branch)
    for i in range(count):

        @pl.when(branch[i] >= 0)
        def _():
            pltpu.make_async_copy(row.at[i], row.at[i], row_sem.at[i]).wait()

    @pl.when(functools.reduce(jnp.maximum, branch) >= 0)
    def _():
        kv = windows[0].shape[2]
        tokens = NPAGE * PAGE * kv
        flat = [
            window[:, :, 0, :].reshape(tokens, 2 * HD) if kv == 1 else window.reshape(tokens, 2 * HD)
            for window in windows
        ]
        query = [row[i, 0] for i in range(count)]
        scores = [
            lax.dot_general(
                query[i], flat[i][:, :HD], (((1,), (1,)), ((), ())), preferred_element_type=jnp.float32
            )
            for i in range(count)
        ]
        token = lax.broadcasted_iota(jnp.int32, scores[0].shape, 1)
        head = lax.broadcasted_iota(jnp.int32, scores[0].shape, 0)
        fits = (token & (kv - 1)) == lax.div(head, H // KVH)
        for i in range(count):
            masked = jnp.where(fits, scores[i], -jnp.inf)
            own = jnp.sum(
                query[i].astype(jnp.float32) * row[i, 1].astype(jnp.float32), -1, keepdims=True
            )
            peak = jnp.maximum(jnp.max(masked, -1, keepdims=True), own)
            terms = jnp.exp(masked - peak)
            own_term = jnp.exp(own - peak)
            total = jnp.sum(terms, -1, keepdims=True) + own_term
            weights = (terms / total).astype(jnp.bfloat16)
            own_weight = (own_term / total).astype(jnp.bfloat16).astype(jnp.float32)
            mixed = jnp.dot(weights, flat[i][:, HD:], preferred_element_type=jnp.float32)
            mixed = mixed + own_weight * row[i, 2].astype(jnp.float32)
            result[i] = mixed.astype(result.dtype)

    for i in range(count):

        @pl.when(branch[i] >= 0)
        def _():
            pltpu.make_async_copy(result.at[i], out.at[branch[i]], out_sem.at[i]).start()

    for i in range(count):

        @pl.when(branch[i] >= 0)
        def _():
            pltpu.make_async_copy(result.at[i], result.at[i], out_sem.at[i]).wait()


def attend_kernel(plan, whom, traced, *refs):
    if traced:
        at, refs = refs[0][0], refs[1:]
        whom = [(at, l) for _, l in whom]
    table, rows, refilled = refs[:3]
    out, window, row, result, sem, row_sem, out_sem = refs[-7:]
    own = [plan.own_taker(table, k) for k in range(KEEP)]
    takers = []
    for _ in range(CAP):
        taker = functools.reduce(jnp.maximum, own)
        own = [jnp.where(other == taker, -1, other) for other in own]
        takers.append(taker)
    branch = []
    for r, i in whom:
        if r is None:
            branch.append(plan.kept(table, i) if i < KEEP else takers[i - KEEP])
        else:
            branch.append(plan.taker(table, r, i))
    for i, who in enumerate(branch):

        @pl.when(who >= 0)
        def _():
            pltpu.make_async_copy(rows.at[who], row.at[i], row_sem.at[i]).start()

            @pl.loop(0, NPAGE, unroll=8)
            def _(p):
                pltpu.make_async_copy(
                    refilled.at[plan.page(table, who, p)], window.at[i, p], sem.at[i]
                ).start()

    for i, who in enumerate(branch):

        @pl.when(who >= 0)
        def _():
            pltpu.make_async_copy(window.at[i], window.at[i], sem.at[i]).wait()

    attend_to(
        branch, [window.at[i] for i in range(len(branch))], row, result, row_sem, out, out_sem
    )


def attend(plan, whom, at, table, rows, refilled, before):
    at = [] if at is None else [jnp.stack([at])]
    count = len(whom)
    heads = rows.shape[2]
    lead = len(at)
    return pl.pallas_call(
        functools.partial(attend_kernel, plan, whom, bool(at)),
        out_shape=jax.ShapeDtypeStruct((rows.shape[0], heads, HD), jnp.bfloat16),
        in_specs=[SMEM] * (lead + 1) + [ANY, HBM] + [ANY] * len(before),
        out_specs=ANY,
        scratch_shapes=[
            pltpu.VMEM((count, NPAGE) + refilled.shape[1:], refilled.dtype),
            pltpu.VMEM((count, 3, heads, HD), rows.dtype),
            pltpu.VMEM((count, heads, HD), jnp.bfloat16),
            pltpu.SemaphoreType.DMA((count,)),
            pltpu.SemaphoreType.DMA((count,)),
            pltpu.SemaphoreType.DMA((count,)),
        ],
        input_output_aliases={lead + 3: 0} if before else {},
        compiler_params=pltpu.CompilerParams(vmem_limit_bytes=ROOM),
        cost_estimate=pl.CostEstimate(
            flops=count * 2 * 2 * 16 * 1536 * 128, bytes_accessed=count * 800_000, transcendentals=0
        ),
        name="attend",
    )(*at, table, rows, refilled, *before)


def token_rows(hidden, w_query, w_key, w_value, query_gain, key_gain):
    features = lax.all_gather(hidden, "mp", axis=1, tiled=True)
    branch_count = features.shape[0]
    head_group = H // KVH
    heads = w_query.shape[1] // HD
    kv_local = w_key.shape[1] // HD
    query_full = jnp.dot(features, w_query, preferred_element_type=jnp.float32)
    query_full = query_full.reshape(branch_count, heads, HD)
    query_rows = (normalize(query_full, query_gain) / math.sqrt(HD)).astype(jnp.bfloat16)
    key_full = jnp.dot(features, w_key, preferred_element_type=jnp.float32)
    key_rows = normalize(key_full.reshape(branch_count, kv_local, HD), key_gain).astype(jnp.bfloat16)
    value_rows = jnp.dot(features, w_value, preferred_element_type=jnp.float32)
    value_rows = value_rows.reshape(branch_count, kv_local, HD).astype(jnp.bfloat16)
    return jnp.stack(
        [
            query_rows,
            jnp.repeat(key_rows, head_group, axis=1),
            jnp.repeat(value_rows, head_group, axis=1),
        ],
        axis=1,
    )


def shards(
    hidden, w_query, w_key, w_value, query_gain, key_gain, kv_pool, page_table, parent, surviving
):
    groups = lax.axis_size("dp")
    me = lax.axis_index("dp")
    ny = groups // NZ
    branch_count = hidden.shape[0]
    links = 2 + ny - 1
    facts = jnp.concatenate(
        [page_table.T, parent[None], surviving[None], jnp.zeros((6, parent.shape[0]), jnp.int32)]
    )
    packed = first_windows(groups, branch_count, facts, kv_pool)
    parent, surviving, page_table, packed = lax.optimization_barrier(
        (parent, surviving, page_table, packed)
    )
    sides = lax.axis_size("mp")

    def everywhere(move):
        return [
            (g * sides + m, to[0] * sides + to[1])
            for g in range(groups)
            for m in range(sides)
            for to in [move(g, m)]
        ]

    def outer(g, m):
        return g + ny if g // ny % 2 == 0 else g - ny, m

    def inner(g, m):
        if g // ny in (0, NZ - 1):
            return g, m ^ 1
        return g + ny if g // ny % 2 else g - ny, m

    def sideways(shift):
        return lambda g, m: (g // ny * ny + (g % ny + shift) % ny, m)

    pairs = [everywhere(outer), everywhere(inner)]
    pairs += [everywhere(sideways(shift)) for shift in range(1, ny)]
    along, beside, every = [0, 1], list(range(2, links)), list(range(links))

    def travel(packed, which):
        return [lax.ppermute(window, ("dp", "mp"), pairs[l]) for window, l in zip(packed, which)]

    arrived = travel(packed, every)
    plan = Plan(links, groups, branch_count)
    table = routing(parent, surviving, page_table, groups, branch_count, links)
    rounds = table[plan.rounds_at]
    refilled, store = own_windows(plan, table, kv_pool, packed[0])
    rows = token_rows(hidden, w_query, w_key, w_value, query_gain, key_gain)
    waiting = [[(None, i) for i in range(3)], [(None, i) for i in range(3, KEEP + CAP)]]
    waiting += [[(r, l) for l in every] for r in range(FIRST)]

    def attend_next(attention):
        return attend(plan, waiting.pop(0), None, table, rows, refilled, attention)

    attention = attend_next([])
    files = [(r, l, 0, NPAGE, l, r * NPAGE) for r in range(FIRST) for l in every]
    store, refilled, attention, packed = step(
        plan,
        [(FIRST, 0, NPAGE, every)],
        [file for file in files if file[1] in along],
        None,
        table,
        arrived[:2],
        kv_pool,
        rows,
        store,
        refilled,
        attention,
        filing=False,
    )
    moved = travel(packed, every)
    for r in range(FIRST, PREFIX):
        if r > FIRST:
            files = [(r - 1, l, 0, NPAGE, l, 0) for l in along]
            files += [(r - 2, l, 0, NPAGE, l, 0) for l in beside if r - 2 >= FIRST]
            arrived = came_along + came_beside
        packs = [(r, 0, NPAGE, beside)] if r > FIRST else []
        packs += [(r + 1, 0, NPAGE, along)] if r + 1 < PREFIX else []
        rest = r + 1 == PREFIX
        store, refilled, attention, packed = step(
            plan, packs, files, None, table, arrived, kv_pool, rows, store, refilled, attention, filing=not rest
        )
        if rest:
            store, refilled, attention, _ = step(
                plan, [], files, None, table, arrived, kv_pool, rows, store, refilled, attention
            )
        if r > FIRST:
            came_along, came_beside = moving_along, moving_beside
            moving_beside = travel(packed[: len(beside)], beside)
            packed = packed[len(beside) :]
            waiting.append([(at, l) for at, l, _, _, _, _ in files])
        else:
            came_along, came_beside, moving_beside = moved[:2], [], moved[2:]
        if packed:
            if came_beside:
                packed, came_beside = lax.optimization_barrier((packed, came_beside))
            moving_along = travel(packed, along)
        for _ in range(2 if len(waiting) > 1 else 1):
            attention = attend_next([attention])
    while waiting:
        attention = attend_next([attention])
    last = PREFIX - 1
    endings = [(last - 1, beside, came_beside), (last, along, came_along), (last, beside, moving_beside)]
    for r, which, arrived in endings:
        files = [(r, l, 0, NPAGE, i, 0) for i, l in enumerate(which)]
        store, refilled, attention, _ = step(
            plan, [], files, None, table, arrived, kv_pool, rows, store, refilled, attention, attending=True
        )

    def more(state):
        return state[0] < rounds

    def one_round(state):
        r, store, refilled, attention = state
        part = NPAGE // PIECES
        moving = []
        for piece in range(PIECES):
            store, refilled, attention, packed = step(
                plan, [(None, piece * part, part, every)], [], r, table, [], kv_pool, rows, store, refilled, attention
            )
            moving.append(travel(packed, every))
        for piece in range(PIECES):
            files = [(None, l, piece * part, part, l, 0) for l in every]
            store, refilled, attention, _ = step(
                plan, [], files, r, table, moving.pop(0), kv_pool, rows, store, refilled, attention
            )
        attention = attend(plan, [(r, l) for l in every], r, table, rows, refilled, [attention])
        return r + 1, store, refilled, attention

    _, store, refilled, attention = lax.while_loop(
        more, one_round, (jnp.int32(PREFIX), store, refilled, attention)
    )
    return (refilled, attention.reshape(branch_count, -1))


def solution(mesh):
    return jax.shard_map(
        shards,
        mesh=mesh,
        in_specs=(
            P("dp", "mp"),
            P(None, "mp"),
            P(None, "mp"),
            P(None, "mp"),
            P(),
            P(),
            P("dp", None, "mp", None),
            P(),
            P(),
            P(),
        ),
        out_specs=(P("dp", None, "mp", None), P("dp", "mp")),
        check_vma=False,
    )
```

profile of v0, /device:TPU:0, one launch (start us, length us, event | category | flops | bytes accessed | tf_op | source)
XLA Modules:
  0.0 162.6 jit_solution(9700143353158485940)
XLA Ops:
  1.8 5.2 %first_windows.1 = (bf16[96,16,2,256]{3,2,1,0:T(2,128)(2,1)}, bf16[96,16,2,256]{3,2,1,0:T(2,128)(2,1)}, bf16[96,16,2,256]{3,2,1,0:T(2,128)(2,1)}) custom-call(s32[56,128]{1,0:T(8,128)S(1)} %add_add_fusion.facts, bf16[768,16,2,256]{3,2,1,0:T(2,128)(2,1)} %refs_2_.3), custom_call_target="tpu_custom_call" | custom-call | bytes 6000000 | tf_op jit(solution)/shard_map/first_windows/pallas_call | solution.py:301
  7.0 3.7 %collective-permute-start.6 = (bf16[96,16,2,256]{3,2,1,0:T(2,128)(2,1)}, bf16[96,16,2,256]{3,2,1,0:T(2,128)(2,1)}, u32[]{:S(2)}, u32[]{:S(2)}) collective-permute-start(bf16[96,16,2,256]{3,2,1,0:T(2,128)(2,1)} %get-tuple-element.144.token), channel_id=1, source_target_pairs={{0,8},{1,9},{2,10},{3,11},{4,12},{5,13},{6,14},{7,15},{8,0},{9,1},... | collective-permute-start | bytes 4718600 | tf_op jit(solution)/shard_map/ppermute | solution.py:703
  11.8 3.5 %plan.1 = s32[48,128]{1,0:T(8,128)S(1)} custom-call(s32[1,128]{1,0:T(1,128)S(1)} %bitcast.38, s32[1,128]{1,0:T(1,128)S(1)} %bitcast.41, s32[128,1]{1,0:T(8,128)S(1)} %copy.68.parent_column, s32[128,1]{1,0:T(8,128)S(1)} %copy.69.alive_column), custom_call_target="tpu_custom_call" | custom-call | bytes 6000000 | tf_op jit(solution)/shard_map/plan/pallas_call | solution.py:196
  16.9 3.4 %own_windows.1 = (bf16[768,16,2,256]{3,2,1,0:T(2,128)(2,1)}, bf16[16,48,16,2,256]{4,3,2,1,0:T(2,128)(2,1)}) custom-call(s32[1153]{0:T(1024)S(1)} %concatenate.7.table.refs_0_, bf16[768,16,2,256]{3,2,1,0:T(2,128)(2,1)} %refs_2_.3, bf16[96,16,2,256]{3,2,1,0:T(2,128)(2,1)} %get-tuple-element.144.token), custom_call_target="tpu_custom_call" | custom-call | bytes 9000000 | tf_op jit(solution)/shard_map/own_windows/pallas_call | solution.py:498
  20.3 5.5 %all_gather.3 = bf16[16,5120]{1,0:T(8,128)(2,1)S(1)} all-gather(bf16[16,1280]{1,0:T(8,128)(2,1)S(1)} %copy-done.5), channel_id=1, replica_groups=mesh['dp'=8,'mp'=4] {'mp'}, dimensions={1}, use_global_device_ids=true | all-gather | bytes 204800 | tf_op jit(solution)/shard_map/all_gather | solution.py:640
  28.5 8.4 %fusion = f32[16,2048]{1,0:T(8,128)S(1)} fusion(bf16[16,5120]{1,0:T(8,128)(2,1)S(1)} %all_gather.3, bf16[5120,2048]{1,0:T(8,128)(2,1)} %param.13), kind=kOutput, calls=%fused_computation.15 | convolution fusion | flops 335544320 | bytes 21266432 | tf_op jit(solution)/shard_map/dot_general | solution.py:645
  38.2 3.9 %attend.10.refs_7_ = bf16[16,16,128]{2,1,0:T(8,128)(2,1)} custom-call(s32[1153]{0:T(1024)S(1)} %concatenate.7.table.refs_0_, bf16[16,3,16,128]{3,2,1,0:T(8,128)(2,1)} %pad_maximum_fusion.refs_1_.refs_4_.refs_5_.refs_3_, bf16[768,16,2,256]{3,2,1,0:T(2,128)(2,1)} %get-tuple-element.147.refs_2_.refs_6_), custom_call_target="tpu_custom_call" | custom-call | flops 37748736 | bytes 2400000 | tf_op jit(solution)/shard_map/attend/pallas_call | solution.py:617
  42.1 3.2 %collective-permute-done.6.refs_1_ = bf16[96,16,2,256]{3,2,1,0:T(2,128)(2,1)} collective-permute-done((bf16[96,16,2,256]{3,2,1,0:T(2,128)(2,1)}, bf16[96,16,2,256]{3,2,1,0:T(2,128)(2,1)}, u32[]{:S(2)}, u32[]{:S(2)}) %collective-permute-start.6) | collective-permute-done | bytes 1572896 | tf_op jit(solution)/shard_map/ppermute | solution.py:703
  47.6 2.3 %collective-permute-start.8 = (bf16[48,16,2,256]{3,2,1,0:T(2,128)(2,1)S(1)}, bf16[48,16,2,256]{3,2,1,0:T(2,128)(2,1)S(1)}, u32[]{:S(2)}, u32[]{:S(2)}) collective-permute-start(bf16[48,16,2,256]{3,2,1,0:T(2,128)(2,1)S(1)} %get-tuple-element.148), channel_id=1, source_target_pairs={{0,8},{1,9},{2,10},{3,11},{4,12},{5,13},{6,14},{7,15},{8,0},{9,1},... | collective-permute-start | bytes 2359304 | tf_op jit(solution)/shard_map/ppermute | solution.py:703
  50.0 2.6 %collective-permute-start.11 = (bf16[48,16,2,256]{3,2,1,0:T(2,128)(2,1)S(1)}, bf16[48,16,2,256]{3,2,1,0:T(2,128)(2,1)S(1)}, u32[]{:S(2)}, u32[]{:S(2)}) collective-permute-start(bf16[48,16,2,256]{3,2,1,0:T(2,128)(2,1)S(1)} %get-tuple-element.159), channel_id=1, source_target_pairs={{0,4},{1,5},{2,6},{3,7},{4,0},{5,1},{6,2},{7,3},{8,12},{9,13},{10,... | collective-permute-start | bytes 2359304 | tf_op jit(solution)/shard_map/ppermute | solution.py:703
  52.6 4.8 %step.16 = (bf16[16,48,16,2,256]{4,3,2,1,0:T(2,128)(2,1)}, bf16[768,16,2,256]{3,2,1,0:T(2,128)(2,1)}, bf16[16,16,128]{2,1,0:T(8,128)(2,1)}, bf16[48,16,2,256]{3,...) custom-call(s32[1153]{0:T(1024)S(1)} %concatenate.7.table.refs_0_, ...), custom_call_target="tpu_custom_call", output_to_operand_aliasing={{0}: (6, {}), {1}: (7, {}), {2}: (8, {})} | custom-call | bytes 6000000 | tf_op jit(solution)/shard_map/step/pallas_call | solution.py:437
  57.4 2.5 %collective-permute-start.14 = (bf16[48,16,2,256]{3,2,1,0:T(2,128)(2,1)S(1)}, bf16[48,16,2,256]{3,2,1,0:T(2,128)(2,1)S(1)}, u32[]{:S(2)}, u32[]{:S(2)}) collective-permute-start(bf16[48,16,2,256]{3,2,1,0:T(2,128)(2,1)S(1)} %get-tuple-element.162), channel_id=1, source_target_pairs={{0,8},{1,9},{2,10},{3,11},{4,12},{5,13},{6,14},{7,15},{8,0},{9,1},... | collective-permute-start | bytes 2359304 | tf_op jit(solution)/shard_map/ppermute | solution.py:703
  59.8 3.9 %attend.11.refs_3_ = bf16[16,16,128]{2,1,0:T(8,128)(2,1)} custom-call(s32[1153]{0:T(1024)S(1)} %concatenate.7.table.refs_0_, bf16[16,3,16,128]{3,2,1,0:T(8,128)(2,1)} %pad_maximum_fusion.refs_1_.refs_4_.refs_5_.refs_3_, bf16[768,16,2,256]{3,2,1,0:T(2,128)(2,1)} %get-tuple-element.155.refs_2_.refs_6_, ...), custom_call_target="tpu_custom_call", output_to_operand_aliasing={{}: (3, {})} | custom-call | flops 37748736 | bytes 2400000 | tf_op jit(solution)/shard_map/attend/pallas_call | solution.py:617
  63.8 3.9 %attend.12.refs_7_ = bf16[16,16,128]{2,1,0:T(8,128)(2,1)} custom-call(s32[1153]{0:T(1024)S(1)} %concatenate.7.table.refs_0_, bf16[16,3,16,128]{3,2,1,0:T(8,128)(2,1)} %pad_maximum_fusion.refs_1_.refs_4_.refs_5_.refs_3_, bf16[768,16,2,256]{3,2,1,0:T(2,128)(2,1)} %get-tuple-element.155.refs_2_.refs_6_, ...), custom_call_target="tpu_custom_call", output_to_operand_aliasing={{}: (3, {})} | custom-call | flops 37748736 | bytes 2400000 | tf_op jit(solution)/shard_map/attend/pallas_call | solution.py:617
  70.8 2.6 %collective-permute-start.16 = (bf16[48,16,2,256]{3,2,1,0:T(2,128)(2,1)S(1)}, bf16[48,16,2,256]{3,2,1,0:T(2,128)(2,1)S(1)}, u32[]{:S(2)}, u32[]{:S(2)}) collective-permute-start(bf16[48,16,2,256]{3,2,1,0:T(2,128)(2,1)S(1)} %get-tuple-element.170), channel_id=1, source_target_pairs={{0,4},{1,5},{2,6},{3,7},{4,0},{5,1},{6,2},{7,3},{8,12},{9,13},{10,... | collective-permute-start | bytes 2359304 | tf_op jit(solution)/shard_map/ppermute | solution.py:703
  73.4 2.4 %collective-permute-start.12 = (bf16[48,16,2,256]{3,2,1,0:T(2,128)(2,1)S(1)}, bf16[48,16,2,256]{3,2,1,0:T(2,128)(2,1)S(1)}, u32[]{:S(2)}, u32[]{:S(2)}) collective-permute-start(bf16[48,16,2,256]{3,2,1,0:T(2,128)(2,1)S(1)} %get-tuple-element.160), channel_id=1, source_target_pairs={{0,8},{1,9},{2,10},{3,11},{4,12},{5,13},{6,14},{7,15},{8,0},{9,1},... | collective-permute-start | bytes 2359304 | tf_op jit(solution)/shard_map/ppermute | solution.py:703
  75.8 3.9 %attend.13.refs_3_ = bf16[16,16,128]{2,1,0:T(8,128)(2,1)} custom-call(s32[1153]{0:T(1024)S(1)} %concatenate.7.table.refs_0_, bf16[16,3,16,128]{3,2,1,0:T(8,128)(2,1)} %pad_maximum_fusion.refs_1_.refs_4_.refs_5_.refs_3_, bf16[768,16,2,256]{3,2,1,0:T(2,128)(2,1)} %get-tuple-element.166.refs_2_.refs_7_, ...), custom_call_target="tpu_custom_call", output_to_operand_aliasing={{}: (3, {})} | custom-call | flops 37748736 | bytes 2400000 | tf_op jit(solution)/shard_map/attend/pallas_call | solution.py:617
  79.7 3.3 %attend.14.refs_8_ = bf16[16,16,128]{2,1,0:T(8,128)(2,1)} custom-call(s32[1153]{0:T(1024)S(1)} %concatenate.7.table.refs_0_, bf16[16,3,16,128]{3,2,1,0:T(8,128)(2,1)} %pad_maximum_fusion.refs_1_.refs_4_.refs_5_.refs_3_, bf16[768,16,2,256]{3,2,1,0:T(2,128)(2,1)} %get-tuple-element.166.refs_2_.refs_7_, ...), custom_call_target="tpu_custom_call", output_to_operand_aliasing={{}: (3, {})} | custom-call | flops 25165824 | bytes 1600000 | tf_op jit(solution)/shard_map/attend/pallas_call | solution.py:617
  85.3 2.3 %step.18 = (bf16[16,48,16,2,256]{4,3,2,1,0:T(2,128)(2,1)}, bf16[768,16,2,256]{3,2,1,0:T(2,128)(2,1)}, bf16[16,16,128]{2,1,0:T(8,128)(2,1)}, bf16[48,16,2,256]{3,...) custom-call(s32[1153]{0:T(1024)S(1)} %concatenate.7.table.refs_0_, ...), custom_call_target="tpu_custom_call", output_to_operand_aliasing={{0}: (6, {}), {1}: (7, {}), {2}: (8, {})} | custom-call | bytes 6000000 | tf_op jit(solution)/shard_map/step/pallas_call | solution.py:437
  87.6 2.5 %collective-permute-start.17 = (bf16[48,16,2,256]{3,2,1,0:T(2,128)(2,1)S(1)}, bf16[48,16,2,256]{3,2,1,0:T(2,128)(2,1)S(1)}, u32[]{:S(2)}, u32[]{:S(2)}) collective-permute-start(bf16[48,16,2,256]{3,2,1,0:T(2,128)(2,1)S(1)} %get-tuple-element.177), channel_id=1, source_target_pairs={{0,4},{1,5},{2,6},{3,7},{4,0},{5,1},{6,2},{7,3},{8,12},{9,13},{10,... | collective-permute-start | bytes 2359304 | tf_op jit(solution)/shard_map/ppermute | solution.py:703
  90.2 3.9 %attend.15.refs_8_ = bf16[16,16,128]{2,1,0:T(8,128)(2,1)} custom-call(s32[1153]{0:T(1024)S(1)} %concatenate.7.table.refs_0_, bf16[16,3,16,128]{3,2,1,0:T(8,128)(2,1)} %pad_maximum_fusion.refs_1_.refs_4_.refs_5_.refs_3_, bf16[768,16,2,256]{3,2,1,0:T(2,128)(2,1)} %get-tuple-element.173.refs_2_.refs_7_, ...), custom_call_target="tpu_custom_call", output_to_operand_aliasing={{}: (3, {})} | custom-call | flops 37748736 | bytes 2400000 | tf_op jit(solution)/shard_map/attend/pallas_call | solution.py:617
  96.0 6.1 %collective-permute-done.12.refs_1_ = bf16[48,16,2,256]{3,2,1,0:T(2,128)(2,1)S(1)} collective-permute-done((bf16[48,16,2,256]{3,2,1,0:T(2,128)(2,1)S(1)}, bf16[48,16,2,256]{3,2,1,0:T(2,128)(2,1)S(1)}, u32[]{:S(2)}, u32[]{:S(2)}) %collective-permute-start.12) | collective-permute-done | bytes 786464 | tf_op jit(solution)/shard_map/ppermute | solution.py:703
  102.1 2.3 %step.19 = (bf16[16,48,16,2,256]{4,3,2,1,0:T(2,128)(2,1)}, bf16[768,16,2,256]{3,2,1,0:T(2,128)(2,1)}, bf16[16,16,128]{2,1,0:T(8,128)(2,1)}, bf16[48,16,2,256]{3,...) custom-call(s32[1153]{0:T(1024)S(1)} %concatenate.7.table.refs_0_, ...), custom_call_target="tpu_custom_call", output_to_operand_aliasing={{0}: (6, {}), {1}: (7, {}), {2}: (8, {})} | custom-call | bytes 6000000 | tf_op jit(solution)/shard_map/step/pallas_call | solution.py:437
  104.5 2.6 %collective-permute-start.22 = (bf16[48,16,2,256]{3,2,1,0:T(2,128)(2,1)S(1)}, bf16[48,16,2,256]{3,2,1,0:T(2,128)(2,1)S(1)}, u32[]{:S(2)}, u32[]{:S(2)}) collective-permute-start(bf16[48,16,2,256]{3,2,1,0:T(2,128)(2,1)S(1)} %get-tuple-element.188), channel_id=1, source_target_pairs={{0,4},{1,5},{2,6},{3,7},{4,0},{5,1},{6,2},{7,3},{8,12},{9,13},{10,... | collective-permute-start | bytes 2359304 | tf_op jit(solution)/shard_map/ppermute | solution.py:703
  109.6 3.9 %attend.16.refs_8_ = bf16[16,16,128]{2,1,0:T(8,128)(2,1)} custom-call(s32[1153]{0:T(1024)S(1)} %concatenate.7.table.refs_0_, bf16[16,3,16,128]{3,2,1,0:T(8,128)(2,1)} %pad_maximum_fusion.refs_1_.refs_4_.refs_5_.refs_3_, bf16[768,16,2,256]{3,2,1,0:T(2,128)(2,1)} %get-tuple-element.184.refs_2_.refs_7_, ...), custom_call_target="tpu_custom_call", output_to_operand_aliasing={{}: (3, {})} | custom-call | flops 37748736 | bytes 2400000 | tf_op jit(solution)/shard_map/attend/pallas_call | solution.py:617
  113.5 5.5 %collective-permute-done.20.refs_1_ = bf16[48,16,2,256]{3,2,1,0:T(2,128)(2,1)S(1)} collective-permute-done((bf16[48,16,2,256]{3,2,1,0:T(2,128)(2,1)S(1)}, bf16[48,16,2,256]{3,2,1,0:T(2,128)(2,1)S(1)}, u32[]{:S(2)}, u32[]{:S(2)}) %collective-permute-start.20) | collective-permute-done | bytes 786464 | tf_op jit(solution)/shard_map/ppermute | solution.py:703
  119.0 3.6 %step.20 = (bf16[16,48,16,2,256]{4,3,2,1,0:T(2,128)(2,1)}, bf16[768,16,2,256]{3,2,1,0:T(2,128)(2,1)}, bf16[16,16,128]{2,1,0:T(8,128)(2,1)}, bf16[48,16,2,256]{3,...) custom-call(s32[1153]{0:T(1024)S(1)} %concatenate.7.table.refs_0_, ...), custom_call_target="tpu_custom_call", output_to_operand_aliasing={{0}: (6, {}), {1}: (7, {}), {2}: (8, {})} | custom-call | bytes 6000000 | tf_op jit(solution)/shard_map/step/pallas_call | solution.py:437
  128.2 7.6 %collective-permute-done.18.refs_1_ = bf16[48,16,2,256]{3,2,1,0:T(2,128)(2,1)S(1)} collective-permute-done((bf16[48,16,2,256]{3,2,1,0:T(2,128)(2,1)S(1)}, bf16[48,16,2,256]{3,2,1,0:T(2,128)(2,1)S(1)}, u32[]{:S(2)}, u32[]{:S(2)}) %collective-permute-start.18) | collective-permute-done | bytes 786464 | tf_op jit(solution)/shard_map/ppermute | solution.py:703
  135.8 2.8 %step.21 = (bf16[16,48,16,2,256]{4,3,2,1,0:T(2,128)(2,1)}, bf16[768,16,2,256]{3,2,1,0:T(2,128)(2,1)}, bf16[16,16,128]{2,1,0:T(8,128)(2,1)}, bf16[48,16,2,256]{3,2,1,0:T(2,128)(2,1)}) custom-call(s32[1153]{0:T(1024)S(1)} %concatenate.7.table.refs_0_, ...), custom_call_target="tpu_custom_call", output_to_operand_aliasing={{0}: (6, {}), {1}: (7, {}), {2}: (8, {})} | custom-call | bytes 6000000 | tf_op jit(solution)/shard_map/step/pallas_call | solution.py:437
  142.3 4.2 %attend.18.refs_6_ = bf16[16,16,128]{2,1,0:T(8,128)(2,1)} custom-call(s32[1153]{0:T(1024)S(1)} %concatenate.7.table.refs_0_, bf16[16,3,16,128]{3,2,1,0:T(8,128)(2,1)} %pad_maximum_fusion.refs_1_.refs_4_.refs_5_.refs_3_, bf16[768,16,2,256]{3,2,1,0:T(2,128)(2,1)} %get-tuple-element.201.refs_2_.refs_5_, ...), custom_call_target="tpu_custom_call", output_to_operand_aliasing={{}: (3, {})} | custom-call | flops 37748736 | bytes 2400000 | tf_op jit(solution)/shard_map/attend/pallas_call | solution.py:617
  146.5 4.2 %step.23 = (bf16[16,48,16,2,256]{4,3,2,1,0:T(2,128)(2,1)}, bf16[768,16,2,256]{3,2,1,0:T(2,128)(2,1)}, bf16[16,16,128]{2,1,0:T(8,128)(2,1)}) custom-call(s32[1153]{0:T(1024)S(1)} %concatenate.7.table.refs_0_, bf16[48,16,2,256]{3,2,1,0:T(2,128)(2,1)} %collective-permute-done.26.refs_1_, ...), custom_call_target="tpu_custom_call", output_to_operand_aliasing={{0}: (4, {}), {1}: (5, {}), {2}: (6, {})} | custom-call | bytes 6000000 | tf_op jit(solution)/shard_map/step/pallas_call | solution.py:437
  152.2 6.8 %collective-permute-done.23.refs_1_ = bf16[48,16,2,256]{3,2,1,0:T(2,128)(2,1)} collective-permute-done((bf16[48,16,2,256]{3,2,1,0:T(2,128)(2,1)}, bf16[48,16,2,256]{3,2,1,0:T(2,128)(2,1)}, u32[]{:S(2)}, u32[]{:S(2)}) %collective-permute-start.23) | collective-permute-done | bytes 786464 | tf_op jit(solution)/shard_map/ppermute | solution.py:703
  (88 shorter events, 34.1 us)
Async XLA Ops:
  0.6 25.2 %copy-start = (bf16[5120,256]{1,0:T(8,128)(2,1)S(1)}, bf16[5120,256]{1,0:T(8,128)(2,1)}, u32[]{:S(2)}) copy-start(bf16[5120,256]{1,0:T(8,128)(2,1)} %param.14) | copy-start | bytes 7864324
  0.6 15.3 %copy-start.4 = (s32[128,48]{0,1:T(8,128)S(1)}, s32[128,48]{0,1:T(8,128)}, u32[]{:S(2)}) copy-start(s32[128,48]{0,1:T(8,128)} %param.19) | copy-start | bytes 73732
  0.7 10.9 %copy-start.2 = (s32[128]{0:T(128)S(1)}, s32[128]{0:T(128)}, u32[]{:S(2)}) copy-start(s32[128]{0:T(128)} %param.20) | copy-start | bytes 1540
  0.7 11.0 %copy-start.3 = (s32[128]{0:T(128)S(1)}, s32[128]{0:T(128)}, u32[]{:S(2)}) copy-start(s32[128]{0:T(128)} %param.21) | copy-start | bytes 1540
  1.8 18.6 %copy-start.5 = (bf16[16,1280]{1,0:T(8,128)(2,1)S(1)}, bf16[16,1280]{1,0:T(8,128)(2,1)}, u32[]{:S(2)}) copy-start(bf16[16,1280]{1,0:T(8,128)(2,1)} %param.12) | copy-start | bytes 122884
  7.0 38.4 %collective-permute-start.6 = (bf16[96,16,2,256]{3,2,1,0:T(2,128)(2,1)}, bf16[96,16,2,256]{3,2,1,0:T(2,128)(2,1)}, u32[]{:S(2)}, u32[]{:S(2)}) collective-permute-start(bf16[96,16,2,256]{3,2,1,0:T(2,128)(2,1)} %get-tuple-element.144.token), channel_id=1, source_target_pairs={{0,8},{1,9},{2,10},{3,11},{4,12},{5,13},{6,14},{7,15},{8,0},{9,1},... | collective-permute-start | bytes 4718600 | tf_op jit(solution)/shard_map/ppermute | solution.py:703
  10.7 34.7 %collective-permute-start.7 = (bf16[96,16,2,256]{3,2,1,0:T(2,128)(2,1)}, bf16[96,16,2,256]{3,2,1,0:T(2,128)(2,1)}, u32[]{:S(2)}, u32[]{:S(2)}) collective-permute-start(bf16[96,16,2,256]{3,2,1,0:T(2,128)(2,1)} %get-tuple-element.145), channel_id=1, source_target_pairs={{0,1},{1,0},{2,3},{3,2},{4,5},{5,4},{6,7},{7,6},{8,16},{9,17},{10,... | collective-permute-start | bytes 4718600 | tf_op jit(solution)/shard_map/ppermute | solution.py:703
  10.7 41.9 %collective-permute-start.10 = (bf16[96,16,2,256]{3,2,1,0:T(2,128)(2,1)}, bf16[96,16,2,256]{3,2,1,0:T(2,128)(2,1)}, u32[]{:S(2)}, u32[]{:S(2)}) collective-permute-start(bf16[96,16,2,256]{3,2,1,0:T(2,128)(2,1)} %get-tuple-element.150), channel_id=1, source_target_pairs={{0,4},{1,5},{2,6},{3,7},{4,0},{5,1},{6,2},{7,3},{8,12},{9,13},{10,... | collective-permute-start | bytes 4718600 | tf_op jit(solution)/shard_map/ppermute | solution.py:703
  28.5 8.8 %copy-start.6 = (f32[128]{0:T(128)S(1)}, f32[128]{0:T(128)}, u32[]{:S(2)}) copy-start(f32[128]{0:T(128)} %param.17) | copy-start | bytes 1540
  28.5 8.9 %copy-start.7 = (f32[128]{0:T(128)S(1)}, f32[128]{0:T(128)}, u32[]{:S(2)}) copy-start(f32[128]{0:T(128)} %param.16) | copy-start | bytes 1540
  47.6 20.8 %collective-permute-start.8 = (bf16[48,16,2,256]{3,2,1,0:T(2,128)(2,1)S(1)}, bf16[48,16,2,256]{3,2,1,0:T(2,128)(2,1)S(1)}, u32[]{:S(2)}, u32[]{:S(2)}) collective-permute-start(bf16[48,16,2,256]{3,2,1,0:T(2,128)(2,1)S(1)} %get-tuple-element.148), channel_id=1, source_target_pairs={{0,8},{1,9},{2,10},{3,11},{4,12},{5,13},{6,14},{7,15},{8,0},{9,1},... | collective-permute-start | bytes 2359304 | tf_op jit(solution)/shard_map/ppermute | solution.py:703
  50.0 18.5 %collective-permute-start.9 = (bf16[48,16,2,256]{3,2,1,0:T(2,128)(2,1)S(1)}, bf16[48,16,2,256]{3,2,1,0:T(2,128)(2,1)S(1)}, u32[]{:S(2)}, u32[]{:S(2)}) collective-permute-start(bf16[48,16,2,256]{3,2,1,0:T(2,128)(2,1)S(1)} %get-tuple-element.149), channel_id=1, source_target_pairs={{0,1},{1,0},{2,3},{3,2},{4,5},{5,4},{6,7},{7,6},{8,16},{9,17},{10,... | collective-permute-start | bytes 2359304 | tf_op jit(solution)/shard_map/ppermute | solution.py:703
  50.0 20.8 %collective-permute-start.11 = (bf16[48,16,2,256]{3,2,1,0:T(2,128)(2,1)S(1)}, bf16[48,16,2,256]{3,2,1,0:T(2,128)(2,1)S(1)}, u32[]{:S(2)}, u32[]{:S(2)}) collective-permute-start(bf16[48,16,2,256]{3,2,1,0:T(2,128)(2,1)S(1)} %get-tuple-element.159), channel_id=1, source_target_pairs={{0,4},{1,5},{2,6},{3,7},{4,0},{5,1},{6,2},{7,3},{8,12},{9,13},{10,... | collective-permute-start | bytes 2359304 | tf_op jit(solution)/shard_map/ppermute | solution.py:703
  57.4 27.9 %collective-permute-start.14 = (bf16[48,16,2,256]{3,2,1,0:T(2,128)(2,1)S(1)}, bf16[48,16,2,256]{3,2,1,0:T(2,128)(2,1)S(1)}, u32[]{:S(2)}, u32[]{:S(2)}) collective-permute-start(bf16[48,16,2,256]{3,2,1,0:T(2,128)(2,1)S(1)} %get-tuple-element.162), channel_id=1, source_target_pairs={{0,8},{1,9},{2,10},{3,11},{4,12},{5,13},{6,14},{7,15},{8,0},{9,1},... | collective-permute-start | bytes 2359304 | tf_op jit(solution)/shard_map/ppermute | solution.py:703
  59.8 25.4 %collective-permute-start.15 = (bf16[48,16,2,256]{3,2,1,0:T(2,128)(2,1)S(1)}, bf16[48,16,2,256]{3,2,1,0:T(2,128)(2,1)S(1)}, u32[]{:S(2)}, u32[]{:S(2)}) collective-permute-start(bf16[48,16,2,256]{3,2,1,0:T(2,128)(2,1)S(1)} %get-tuple-element.163), channel_id=1, source_target_pairs={{0,1},{1,0},{2,3},{3,2},{4,5},{5,4},{6,7},{7,6},{8,16},{9,17},{10,... | collective-permute-start | bytes 2359304 | tf_op jit(solution)/shard_map/ppermute | solution.py:703
  70.8 23.3 %collective-permute-start.16 = (bf16[48,16,2,256]{3,2,1,0:T(2,128)(2,1)S(1)}, bf16[48,16,2,256]{3,2,1,0:T(2,128)(2,1)S(1)}, u32[]{:S(2)}, u32[]{:S(2)}) collective-permute-start(bf16[48,16,2,256]{3,2,1,0:T(2,128)(2,1)S(1)} %get-tuple-element.170), channel_id=1, source_target_pairs={{0,4},{1,5},{2,6},{3,7},{4,0},{5,1},{6,2},{7,3},{8,12},{9,13},{10,... | collective-permute-start | bytes 2359304 | tf_op jit(solution)/shard_map/ppermute | solution.py:703
  73.4 28.7 %collective-permute-start.12 = (bf16[48,16,2,256]{3,2,1,0:T(2,128)(2,1)S(1)}, bf16[48,16,2,256]{3,2,1,0:T(2,128)(2,1)S(1)}, u32[]{:S(2)}, u32[]{:S(2)}) collective-permute-start(bf16[48,16,2,256]{3,2,1,0:T(2,128)(2,1)S(1)} %get-tuple-element.160), channel_id=1, source_target_pairs={{0,8},{1,9},{2,10},{3,11},{4,12},{5,13},{6,14},{7,15},{8,0},{9,1},... | collective-permute-start | bytes 2359304 | tf_op jit(solution)/shard_map/ppermute | solution.py:703
  75.8 26.3 %collective-permute-start.13 = (bf16[48,16,2,256]{3,2,1,0:T(2,128)(2,1)S(1)}, bf16[48,16,2,256]{3,2,1,0:T(2,128)(2,1)S(1)}, u32[]{:S(2)}, u32[]{:S(2)}) collective-permute-start(bf16[48,16,2,256]{3,2,1,0:T(2,128)(2,1)S(1)} %get-tuple-element.161), channel_id=1, source_target_pairs={{0,1},{1,0},{2,3},{3,2},{4,5},{5,4},{6,7},{7,6},{8,16},{9,17},{10,... | collective-permute-start | bytes 2359304 | tf_op jit(solution)/shard_map/ppermute | solution.py:703
  87.6 21.0 %collective-permute-start.17 = (bf16[48,16,2,256]{3,2,1,0:T(2,128)(2,1)S(1)}, bf16[48,16,2,256]{3,2,1,0:T(2,128)(2,1)S(1)}, u32[]{:S(2)}, u32[]{:S(2)}) collective-permute-start(bf16[48,16,2,256]{3,2,1,0:T(2,128)(2,1)S(1)} %get-tuple-element.177), channel_id=1, source_target_pairs={{0,4},{1,5},{2,6},{3,7},{4,0},{5,1},{6,2},{7,3},{8,12},{9,13},{10,... | collective-permute-start | bytes 2359304 | tf_op jit(solution)/shard_map/ppermute | solution.py:703
  94.1 24.9 %collective-permute-start.20 = (bf16[48,16,2,256]{3,2,1,0:T(2,128)(2,1)S(1)}, bf16[48,16,2,256]{3,2,1,0:T(2,128)(2,1)S(1)}, u32[]{:S(2)}, u32[]{:S(2)}) collective-permute-start(bf16[48,16,2,256]{3,2,1,0:T(2,128)(2,1)S(1)} %get-tuple-element.180), channel_id=1, source_target_pairs={{0,8},{1,9},{2,10},{3,11},{4,12},{5,13},{6,14},{7,15},{8,0},{9,1},... | collective-permute-start | bytes 2359304 | tf_op jit(solution)/shard_map/ppermute | solution.py:703
  96.0 23.0 %collective-permute-start.21 = (bf16[48,16,2,256]{3,2,1,0:T(2,128)(2,1)S(1)}, bf16[48,16,2,256]{3,2,1,0:T(2,128)(2,1)S(1)}, u32[]{:S(2)}, u32[]{:S(2)}) collective-permute-start(bf16[48,16,2,256]{3,2,1,0:T(2,128)(2,1)S(1)} %get-tuple-element.181), channel_id=1, source_target_pairs={{0,1},{1,0},{2,3},{3,2},{4,5},{5,4},{6,7},{7,6},{8,16},{9,17},{10,... | collective-permute-start | bytes 2359304 | tf_op jit(solution)/shard_map/ppermute | solution.py:703
  104.5 19.4 %collective-permute-start.22 = (bf16[48,16,2,256]{3,2,1,0:T(2,128)(2,1)S(1)}, bf16[48,16,2,256]{3,2,1,0:T(2,128)(2,1)S(1)}, u32[]{:S(2)}, u32[]{:S(2)}) collective-permute-start(bf16[48,16,2,256]{3,2,1,0:T(2,128)(2,1)S(1)} %get-tuple-element.188), channel_id=1, source_target_pairs={{0,4},{1,5},{2,6},{3,7},{4,0},{5,1},{6,2},{7,3},{8,12},{9,13},{10,... | collective-permute-start | bytes 2359304 | tf_op jit(solution)/shard_map/ppermute | solution.py:703
  108.6 27.2 %collective-permute-start.18 = (bf16[48,16,2,256]{3,2,1,0:T(2,128)(2,1)S(1)}, bf16[48,16,2,256]{3,2,1,0:T(2,128)(2,1)S(1)}, u32[]{:S(2)}, u32[]{:S(2)}) collective-permute-start(bf16[48,16,2,256]{3,2,1,0:T(2,128)(2,1)S(1)} %get-tuple-element.178), channel_id=1, source_target_pairs={{0,8},{1,9},{2,10},{3,11},{4,12},{5,13},{6,14},{7,15},{8,0},{9,1},... | collective-permute-start | bytes 2359304 | tf_op jit(solution)/shard_map/ppermute | solution.py:703
  109.6 26.2 %collective-permute-start.19 = (bf16[48,16,2,256]{3,2,1,0:T(2,128)(2,1)S(1)}, bf16[48,16,2,256]{3,2,1,0:T(2,128)(2,1)S(1)}, u32[]{:S(2)}, u32[]{:S(2)}) collective-permute-start(bf16[48,16,2,256]{3,2,1,0:T(2,128)(2,1)S(1)} %get-tuple-element.179), channel_id=1, source_target_pairs={{0,1},{1,0},{2,3},{3,2},{4,5},{5,4},{6,7},{7,6},{8,16},{9,17},{10,... | collective-permute-start | bytes 2359304 | tf_op jit(solution)/shard_map/ppermute | solution.py:703
  123.9 22.6 %collective-permute-start.26 = (bf16[48,16,2,256]{3,2,1,0:T(2,128)(2,1)}, bf16[48,16,2,256]{3,2,1,0:T(2,128)(2,1)}, u32[]{:S(2)}, u32[]{:S(2)}) collective-permute-start(bf16[48,16,2,256]{3,2,1,0:T(2,128)(2,1)} %get-tuple-element.196), channel_id=1, source_target_pairs={{0,4},{1,5},{2,6},{3,7},{4,0},{5,1},{6,2},{7,3},{8,12},{9,13},{10,... | collective-permute-start | bytes 2359304 | tf_op jit(solution)/shard_map/ppermute | solution.py:703
  125.4 25.5 %collective-permute-start.24 = (bf16[48,16,2,256]{3,2,1,0:T(2,128)(2,1)}, bf16[48,16,2,256]{3,2,1,0:T(2,128)(2,1)S(1)}, u32[]{:S(2)}, u32[]{:S(2)}) collective-permute-start(bf16[48,16,2,256]{3,2,1,0:T(2,128)(2,1)} %get-tuple-element.194), channel_id=1, source_target_pairs={{0,8},{1,9},{2,10},{3,11},{4,12},{5,13},{6,14},{7,15},{8,0},{9,1},... | collective-permute-start | bytes 2359304 | tf_op jit(solution)/shard_map/ppermute | solution.py:703
  128.1 22.8 %collective-permute-start.25 = (bf16[48,16,2,256]{3,2,1,0:T(2,128)(2,1)}, bf16[48,16,2,256]{3,2,1,0:T(2,128)(2,1)}, u32[]{:S(2)}, u32[]{:S(2)}) collective-permute-start(bf16[48,16,2,256]{3,2,1,0:T(2,128)(2,1)} %get-tuple-element.195), channel_id=1, source_target_pairs={{0,1},{1,0},{2,3},{3,2},{4,5},{5,4},{6,7},{7,6},{8,16},{9,17},{10,... | collective-permute-start | bytes 2359304 | tf_op jit(solution)/shard_map/ppermute | solution.py:703
  138.6 20.3 %collective-permute-start.23 = (bf16[48,16,2,256]{3,2,1,0:T(2,128)(2,1)}, bf16[48,16,2,256]{3,2,1,0:T(2,128)(2,1)}, u32[]{:S(2)}, u32[]{:S(2)}) collective-permute-start(bf16[48,16,2,256]{3,2,1,0:T(2,128)(2,1)} %get-tuple-element.193), channel_id=1, source_target_pairs={{0,4},{1,5},{2,6},{3,7},{4,0},{5,1},{6,2},{7,3},{8,12},{9,13},{10,... | collective-permute-start | bytes 2359304 | tf_op jit(solution)/shard_map/ppermute | solution.py:703
  142.3 8.6 %slice-start = ((s8[12582912]{0:T(1024)(128)(4,1)}), s8[4194304]{0:T(1024)(128)(4,1)S(1)}, s32[]{:S(2)}) async-start(s8[12582912]{0:T(1024)(128)(4,1)} %bitcast.42), calls=%async_computation | async-start | bytes 8388608
  146.5 4.4 %slice-start.1 = ((s8[12582912]{0:T(1024)(128)(4,1)}), s8[4194304]{0:T(1024)(128)(4,1)S(1)}, s32[]{:S(2)}) async-start(s8[12582912]{0:T(1024)(128)(4,1)} %bitcast.42), calls=%async_computation.1 | async-start | bytes 8388608
  146.5 4.4 %slice-start.2 = ((s8[12582912]{0:T(1024)(128)(4,1)}), s8[4194304]{0:T(1024)(128)(4,1)S(1)}, s32[]{:S(2)}) async-start(s8[12582912]{0:T(1024)(128)(4,1)} %bitcast.42), calls=%async_computation.2 | async-start | bytes 8388608
  160.8 1.8 %copy-start.1 = (bf16[5120,256]{1,0:T(8,128)(2,1)S(1)}, bf16[5120,256]{1,0:T(8,128)(2,1)}, u32[]{:S(2)}) copy-start(bf16[5120,256]{1,0:T(8,128)(2,1)} %param.14) | copy-start | bytes 7864324
where the time goes:
time: 164 us; the launch traced here: 163 us
  Pallas kernels  72.9 us (44%)
  waiting for transfers between devices  35.2 us (21%)
  starting transfers between devices  30.2 us (18%)
  matrix products  11.1 us (7%)
  blocking collectives  5.52 us (3%)
  local copies, waits for them, and re-layouts  3.82 us (2%)
  other arithmetic  2.09 us (1%)
    ppermute x21, waiting for transfers between devices, travel(): lax.ppermute(window, ('dp', 'mp'), pairs[l])  35.2 us
    pallas_call x9, Pallas kernels, attend(): pl.pallas_call(functools.partial(attend_kernel, plan, whom, bool(at)), ou...  31.5 us
    ppermute x21, starting transfers between devices, travel(): lax.ppermute(window, ('dp', 'mp'), pairs[l])  30.2 us
    pallas_call x11, Pallas kernels, step(): pl.pallas_call(functools.partial(step_kernel, plan, packs, files, bool(at...  29.3 us
    dot_general x1, matrix products, token_rows(): query_full = jnp.dot(features, w_query, preferred_element_type=jnp.float32)  8.44 us
    all_gather x1, blocking collectives, token_rows(): features = lax.all_gather(hidden, 'mp', axis=1, tiled=True)  5.52 us
    pallas_call x1, Pallas kernels, first_windows(): pl.pallas_call(functools.partial(first_kernel, groups, branch_count), out...  5.21 us
    pallas_call x1, Pallas kernels, routing(): pl.pallas_call(functools.partial(plan_kernel, groups, branch_count), out_...  3.5 us
  transfers between devices with their start and end apart: 21, of which 10 were waited for; matrix products, arithmetic and copies ran while one was open for 9% of the time, Pallas kernels for 41%

commit v1 on v0

--- a/solution.py
+++ b/solution.py
@@ -22,7 +22,9 @@
 FIRST = 2
 REST = 2
 PIECES = 2
-ROOM = 48 * 1024 * 1024
+LITTLE = 24 * 1024 * 1024
+ROOM = 44 * 1024 * 1024
+MUCH = 52 * 1024 * 1024
 NEVER = 1 << 20
 
 
@@ -199,7 +201,7 @@
         in_specs=[VMEM] * 4,
         out_specs=VMEM,
         scratch_shapes=[pltpu.VMEM((2 * rows, groups, LANES), jnp.int32)],
-        compiler_params=pltpu.CompilerParams(vmem_limit_bytes=ROOM),
+        compiler_params=pltpu.CompilerParams(vmem_limit_bytes=LITTLE),
         cost_estimate=pl.CostEstimate(flops=0, bytes_accessed=6_000_000, transcendentals=0),
         name="plan",
     )(
@@ -308,7 +310,7 @@
             pltpu.SemaphoreType.DMA,
             pltpu.SemaphoreType.DMA((links, FIRST)),
         ],
-        compiler_params=pltpu.CompilerParams(vmem_limit_bytes=ROOM),
+        compiler_params=pltpu.CompilerParams(vmem_limit_bytes=LITTLE),
         cost_estimate=pl.CostEstimate(flops=0, bytes_accessed=6_000_000, transcendentals=0),
         name="first_windows",
     )(facts, pool)
@@ -449,7 +451,7 @@
         + [pltpu.SemaphoreType.DMA((some,))] * 4
         + [pltpu.SemaphoreType.DMA((max(len(boxes), 1),))] * 2,
         input_output_aliases={lead + 2: 0, lead + 3: 1, lead + 4: 2},
-        compiler_params=pltpu.CompilerParams(vmem_limit_bytes=ROOM),
+        compiler_params=pltpu.CompilerParams(vmem_limit_bytes=MUCH if attending or at else ROOM),
         cost_estimate=pl.CostEstimate(flops=0, bytes_accessed=6_000_000, transcendentals=0),
         name="step",
     )(*at, table, *arrived, pool, rows, store, refilled, attention)

time: 164 us -> 164 us (level)
  waiting for transfers between devices: 35.2 us -> 42.3 us
  starting transfers between devices: 30.2 us -> 25.7 us
  Pallas kernels: 72.9 us -> 68.9 us
    ppermute x21, waiting for transfers between devices: 35.2 us -> 42.3 us  [travel(): lax.ppermute(window, ('dp', 'mp'), pairs[l])]
    ppermute x21, starting transfers between devices: 30.2 us -> 25.7 us  [travel(): lax.ppermute(window, ('dp', 'mp'), pairs[l])]
    pallas_call x9, Pallas kernels: 31.5 us -> 28.6 us  [attend(): pl.pallas_call(functools.partial(attend_kernel, plan, whom, bool(at)), ou...]
  transfers between devices with their start and end apart: 21 -> 21, of which waited for: 10 -> 10; matrix products, arithmetic and copies ran while one was open for 9% -> 9% of each run, Pallas kernels for 41% -> 39%
where the time goes in v1:
time: 164 us; the launch traced here: 161 us
  Pallas kernels  68.9 us (42%)
  waiting for transfers between devices  42.3 us (26%)
  starting transfers between devices  25.7 us (16%)
  matrix products  11.1 us (7%)
  blocking collectives  5.52 us (3%)
  local copies, waits for them, and re-layouts  3.8 us (2%)
  other arithmetic  2.11 us (1%)
    ppermute x21, waiting for transfers between devices, travel(): lax.ppermute(window, ('dp', 'mp'), pairs[l])  42.3 us
    pallas_call x9, Pallas kernels, attend(): pl.pallas_call(functools.partial(attend_kernel, plan, whom, bool(at)), ou...  28.6 us
    pallas_call x11, Pallas kernels, step(): pl.pallas_call(functools.partial(step_kernel, plan, packs, files, bool(at...  28.1 us
    ppermute x21, starting transfers between devices, travel(): lax.ppermute(window, ('dp', 'mp'), pairs[l])  25.7 us
    dot_general x1, matrix products, token_rows(): query_full = jnp.dot(features, w_query, preferred_element_type=jnp.float32)  8.44 us
    all_gather x1, blocking collectives, token_rows(): features = lax.all_gather(hidden, 'mp', axis=1, tiled=True)  5.52 us
    pallas_call x1, Pallas kernels, first_windows(): pl.pallas_call(functools.partial(first_kernel, groups, branch_count), out...  5.13 us
    pallas_call x1, Pallas kernels, routing(): pl.pallas_call(functools.partial(plan_kernel, groups, branch_count), out_...  3.5 us
  transfers between devices with their start and end apart: 21, of which 10 were waited for; matrix products, arithmetic and copies ran while one was open for 9% of the time, Pallas kernels for 39%

profile of v1, /device:TPU:0, one launch (start us, length us, event | category | flops | bytes accessed | tf_op | source)
XLA Modules:
  0.0 161.0 jit_solution(15912158172932948248)
XLA Ops:
  1.8 5.1 %first_windows.1 = (bf16[96,16,2,256]{3,2,1,0:T(2,128)(2,1)}, bf16[96,16,2,256]{3,2,1,0:T(2,128)(2,1)}, bf16[96,16,2,256]{3,2,1,0:T(2,128)(2,1)}) custom-call(s32[56,128]{1,0:T(8,128)S(1)} %add_add_fusion.facts, bf16[768,16,2,256]{3,2,1,0:T(2,128)(2,1)} %refs_2_.3), custom_call_target="tpu_custom_call" | custom-call | bytes 6000000 | tf_op jit(solution)/shard_map/first_windows/pallas_call | solution.py:303
  6.9 3.6 %collective-permute-start.6 = (bf16[96,16,2,256]{3,2,1,0:T(2,128)(2,1)}, bf16[96,16,2,256]{3,2,1,0:T(2,128)(2,1)}, u32[]{:S(2)}, u32[]{:S(2)}) collective-permute-start(bf16[96,16,2,256]{3,2,1,0:T(2,128)(2,1)} %get-tuple-element.144.token), channel_id=1, source_target_pairs={{0,8},{1,9},{2,10},{3,11},{4,12},{5,13},{6,14},{7,15},{8,0},{9,1},... | collective-permute-start | bytes 4718600 | tf_op jit(solution)/shard_map/ppermute | solution.py:705
  11.8 3.5 %plan.1 = s32[48,128]{1,0:T(8,128)S(1)} custom-call(s32[1,128]{1,0:T(1,128)S(1)} %bitcast.38, s32[1,128]{1,0:T(1,128)S(1)} %bitcast.41, s32[128,1]{1,0:T(8,128)S(1)} %copy.68.parent_column, s32[128,1]{1,0:T(8,128)S(1)} %copy.69.alive_column), custom_call_target="tpu_custom_call" | custom-call | bytes 6000000 | tf_op jit(solution)/shard_map/plan/pallas_call | solution.py:198
  16.9 3.4 %own_windows.1 = (bf16[768,16,2,256]{3,2,1,0:T(2,128)(2,1)}, bf16[16,48,16,2,256]{4,3,2,1,0:T(2,128)(2,1)}) custom-call(s32[1153]{0:T(1024)S(1)} %concatenate.7.table.refs_0_, bf16[768,16,2,256]{3,2,1,0:T(2,128)(2,1)} %refs_2_.3, bf16[96,16,2,256]{3,2,1,0:T(2,128)(2,1)} %get-tuple-element.144.token), custom_call_target="tpu_custom_call" | custom-call | bytes 9000000 | tf_op jit(solution)/shard_map/own_windows/pallas_call | solution.py:500
  20.4 5.5 %all_gather.3 = bf16[16,5120]{1,0:T(8,128)(2,1)S(1)} all-gather(bf16[16,1280]{1,0:T(8,128)(2,1)S(1)} %copy-done.5), channel_id=1, replica_groups=mesh['dp'=8,'mp'=4] {'mp'}, dimensions={1}, use_global_device_ids=true | all-gather | bytes 204800 | tf_op jit(solution)/shard_map/all_gather | solution.py:642
  28.6 8.4 %fusion = f32[16,2048]{1,0:T(8,128)S(1)} fusion(bf16[16,5120]{1,0:T(8,128)(2,1)S(1)} %all_gather.3, bf16[5120,2048]{1,0:T(8,128)(2,1)} %param.13), kind=kOutput, calls=%fused_computation.15 | convolution fusion | flops 335544320 | bytes 21266432 | tf_op jit(solution)/shard_map/dot_general | solution.py:647
  38.3 3.9 %attend.10.refs_7_ = bf16[16,16,128]{2,1,0:T(8,128)(2,1)} custom-call(s32[1153]{0:T(1024)S(1)} %concatenate.7.table.refs_0_, bf16[16,3,16,128]{3,2,1,0:T(8,128)(2,1)} %pad_maximum_fusion.refs_1_.refs_4_.refs_5_.refs_3_, bf16[768,16,2,256]{3,2,1,0:T(2,128)(2,1)} %get-tuple-element.147.refs_2_.refs_6_), custom_call_target="tpu_custom_call" | custom-call | flops 37748736 | bytes 2400000 | tf_op jit(solution)/shard_map/attend/pallas_call | solution.py:619
  42.2 3.0 %collective-permute-done.6.refs_1_ = bf16[96,16,2,256]{3,2,1,0:T(2,128)(2,1)} collective-permute-done((bf16[96,16,2,256]{3,2,1,0:T(2,128)(2,1)}, bf16[96,16,2,256]{3,2,1,0:T(2,128)(2,1)}, u32[]{:S(2)}, u32[]{:S(2)}) %collective-permute-start.6) | collective-permute-done | bytes 1572896 | tf_op jit(solution)/shard_map/ppermute | solution.py:705
  45.2 2.2 %step.15 = (bf16[16,48,16,2,256]{4,3,2,1,0:T(2,128)(2,1)}, bf16[768,16,2,256]{3,2,1,0:T(2,128)(2,1)}, bf16[16,16,128]{2,1,0:T(8,128)(2,1)}, bf16[48,16,2,256]{3,...) custom-call(s32[1153]{0:T(1024)S(1)} %concatenate.7.table.refs_0_, ...), custom_call_target="tpu_custom_call", output_to_operand_aliasing={{0}: (5, {}), {1}: (6, {}), {2}: (7, {})} | custom-call | bytes 6000000 | tf_op jit(solution)/shard_map/step/pallas_call | solution.py:439
  47.5 2.5 %collective-permute-start.8 = (bf16[48,16,2,256]{3,2,1,0:T(2,128)(2,1)S(1)}, bf16[48,16,2,256]{3,2,1,0:T(2,128)(2,1)S(1)}, u32[]{:S(2)}, u32[]{:S(2)}) collective-permute-start(bf16[48,16,2,256]{3,2,1,0:T(2,128)(2,1)S(1)} %get-tuple-element.148), channel_id=1, source_target_pairs={{0,8},{1,9},{2,10},{3,11},{4,12},{5,13},{6,14},{7,15},{8,0},{9,1},... | collective-permute-start | bytes 2359304 | tf_op jit(solution)/shard_map/ppermute | solution.py:705
  51.0 4.8 %step.16 = (bf16[16,48,16,2,256]{4,3,2,1,0:T(2,128)(2,1)}, bf16[768,16,2,256]{3,2,1,0:T(2,128)(2,1)}, bf16[16,16,128]{2,1,0:T(8,128)(2,1)}, bf16[48,16,2,256]{3,...) custom-call(s32[1153]{0:T(1024)S(1)} %concatenate.7.table.refs_0_, ...), custom_call_target="tpu_custom_call", output_to_operand_aliasing={{0}: (6, {}), {1}: (7, {}), {2}: (8, {})} | custom-call | bytes 6000000 | tf_op jit(solution)/shard_map/step/pallas_call | solution.py:439
  55.8 2.4 %collective-permute-start.14 = (bf16[48,16,2,256]{3,2,1,0:T(2,128)(2,1)S(1)}, bf16[48,16,2,256]{3,2,1,0:T(2,128)(2,1)S(1)}, u32[]{:S(2)}, u32[]{:S(2)}) collective-permute-start(bf16[48,16,2,256]{3,2,1,0:T(2,128)(2,1)S(1)} %get-tuple-element.162), channel_id=1, source_target_pairs={{0,8},{1,9},{2,10},{3,11},{4,12},{5,13},{6,14},{7,15},{8,0},{9,1},... | collective-permute-start | bytes 2359304 | tf_op jit(solution)/shard_map/ppermute | solution.py:705
  58.3 3.9 %attend.11.refs_3_ = bf16[16,16,128]{2,1,0:T(8,128)(2,1)} custom-call(s32[1153]{0:T(1024)S(1)} %concatenate.7.table.refs_0_, bf16[16,3,16,128]{3,2,1,0:T(8,128)(2,1)} %pad_maximum_fusion.refs_1_.refs_4_.refs_5_.refs_3_, bf16[768,16,2,256]{3,2,1,0:T(2,128)(2,1)} %get-tuple-element.155.refs_2_.refs_6_, ...), custom_call_target="tpu_custom_call", output_to_operand_aliasing={{}: (3, {})} | custom-call | flops 37748736 | bytes 2400000 | tf_op jit(solution)/shard_map/attend/pallas_call | solution.py:619
  62.2 3.9 %attend.12.refs_7_ = bf16[16,16,128]{2,1,0:T(8,128)(2,1)} custom-call(s32[1153]{0:T(1024)S(1)} %concatenate.7.table.refs_0_, bf16[16,3,16,128]{3,2,1,0:T(8,128)(2,1)} %pad_maximum_fusion.refs_1_.refs_4_.refs_5_.refs_3_, bf16[768,16,2,256]{3,2,1,0:T(2,128)(2,1)} %get-tuple-element.155.refs_2_.refs_6_, ...), custom_call_target="tpu_custom_call", output_to_operand_aliasing={{}: (3, {})} | custom-call | flops 37748736 | bytes 2400000 | tf_op jit(solution)/shard_map/attend/pallas_call | solution.py:619
  66.1 2.4 %collective-permute-done.8.refs_1_ = bf16[48,16,2,256]{3,2,1,0:T(2,128)(2,1)S(1)} collective-permute-done((bf16[48,16,2,256]{3,2,1,0:T(2,128)(2,1)S(1)}, bf16[48,16,2,256]{3,2,1,0:T(2,128)(2,1)S(1)}, u32[]{:S(2)}, u32[]{:S(2)}) %collective-permute-start.8) | collective-permute-done | bytes 786464 | tf_op jit(solution)/shard_map/ppermute | solution.py:705
  70.2 2.3 %collective-permute-start.16 = (bf16[48,16,2,256]{3,2,1,0:T(2,128)(2,1)S(1)}, bf16[48,16,2,256]{3,2,1,0:T(2,128)(2,1)S(1)}, u32[]{:S(2)}, u32[]{:S(2)}) collective-permute-start(bf16[48,16,2,256]{3,2,1,0:T(2,128)(2,1)S(1)} %get-tuple-element.170), channel_id=1, source_target_pairs={{0,4},{1,5},{2,6},{3,7},{4,0},{5,1},{6,2},{7,3},{8,12},{9,13},{10,... | collective-permute-start | bytes 2359304 | tf_op jit(solution)/shard_map/ppermute | solution.py:705
  74.4 3.9 %attend.13.refs_3_ = bf16[16,16,128]{2,1,0:T(8,128)(2,1)} custom-call(s32[1153]{0:T(1024)S(1)} %concatenate.7.table.refs_0_, bf16[16,3,16,128]{3,2,1,0:T(8,128)(2,1)} %pad_maximum_fusion.refs_1_.refs_4_.refs_5_.refs_3_, bf16[768,16,2,256]{3,2,1,0:T(2,128)(2,1)} %get-tuple-element.166.refs_2_.refs_7_, ...), custom_call_target="tpu_custom_call", output_to_operand_aliasing={{}: (3, {})} | custom-call | flops 37748736 | bytes 2400000 | tf_op jit(solution)/shard_map/attend/pallas_call | solution.py:619
  79.0 6.3 %collective-permute-done.14.refs_1_ = bf16[48,16,2,256]{3,2,1,0:T(2,128)(2,1)S(1)} collective-permute-done((bf16[48,16,2,256]{3,2,1,0:T(2,128)(2,1)S(1)}, bf16[48,16,2,256]{3,2,1,0:T(2,128)(2,1)S(1)}, u32[]{:S(2)}, u32[]{:S(2)}) %collective-permute-start.14) | collective-permute-done | bytes 786464 | tf_op jit(solution)/shard_map/ppermute | solution.py:705
  85.3 2.3 %step.18 = (bf16[16,48,16,2,256]{4,3,2,1,0:T(2,128)(2,1)}, bf16[768,16,2,256]{3,2,1,0:T(2,128)(2,1)}, bf16[16,16,128]{2,1,0:T(8,128)(2,1)}, bf16[48,16,2,256]{3,...) custom-call(s32[1153]{0:T(1024)S(1)} %concatenate.7.table.refs_0_, ...), custom_call_target="tpu_custom_call", output_to_operand_aliasing={{0}: (6, {}), {1}: (7, {}), {2}: (8, {})} | custom-call | bytes 6000000 | tf_op jit(solution)/shard_map/step/pallas_call | solution.py:439
  89.0 3.9 %attend.15.refs_8_ = bf16[16,16,128]{2,1,0:T(8,128)(2,1)} custom-call(s32[1153]{0:T(1024)S(1)} %concatenate.7.table.refs_0_, bf16[16,3,16,128]{3,2,1,0:T(8,128)(2,1)} %pad_maximum_fusion.refs_1_.refs_4_.refs_5_.refs_3_, bf16[768,16,2,256]{3,2,1,0:T(2,128)(2,1)} %get-tuple-element.173.refs_2_.refs_7_, ...), custom_call_target="tpu_custom_call", output_to_operand_aliasing={{}: (3, {})} | custom-call | flops 37748736 | bytes 2400000 | tf_op jit(solution)/shard_map/attend/pallas_call | solution.py:619
  92.9 2.4 %collective-permute-start.20 = (bf16[48,16,2,256]{3,2,1,0:T(2,128)(2,1)S(1)}, bf16[48,16,2,256]{3,2,1,0:T(2,128)(2,1)S(1)}, u32[]{:S(2)}, u32[]{:S(2)}) collective-permute-start(bf16[48,16,2,256]{3,2,1,0:T(2,128)(2,1)S(1)} %get-tuple-element.180), channel_id=1, source_target_pairs={{0,8},{1,9},{2,10},{3,11},{4,12},{5,13},{6,14},{7,15},{8,0},{9,1},... | collective-permute-start | bytes 2359304 | tf_op jit(solution)/shard_map/ppermute | solution.py:705
  95.3 6.9 %collective-permute-done.12.refs_1_ = bf16[48,16,2,256]{3,2,1,0:T(2,128)(2,1)S(1)} collective-permute-done((bf16[48,16,2,256]{3,2,1,0:T(2,128)(2,1)S(1)}, bf16[48,16,2,256]{3,2,1,0:T(2,128)(2,1)S(1)}, u32[]{:S(2)}, u32[]{:S(2)}) %collective-permute-start.12) | collective-permute-done | bytes 786464 | tf_op jit(solution)/shard_map/ppermute | solution.py:705
  102.1 2.3 %step.19 = (bf16[16,48,16,2,256]{4,3,2,1,0:T(2,128)(2,1)}, bf16[768,16,2,256]{3,2,1,0:T(2,128)(2,1)}, bf16[16,16,128]{2,1,0:T(8,128)(2,1)}, bf16[48,16,2,256]{3,...) custom-call(s32[1153]{0:T(1024)S(1)} %concatenate.7.table.refs_0_, ...), custom_call_target="tpu_custom_call", output_to_operand_aliasing={{0}: (6, {}), {1}: (7, {}), {2}: (8, {})} | custom-call | bytes 6000000 | tf_op jit(solution)/shard_map/step/pallas_call | solution.py:439
  108.1 3.9 %attend.16.refs_8_ = bf16[16,16,128]{2,1,0:T(8,128)(2,1)} custom-call(s32[1153]{0:T(1024)S(1)} %concatenate.7.table.refs_0_, bf16[16,3,16,128]{3,2,1,0:T(8,128)(2,1)} %pad_maximum_fusion.refs_1_.refs_4_.refs_5_.refs_3_, bf16[768,16,2,256]{3,2,1,0:T(2,128)(2,1)} %get-tuple-element.184.refs_2_.refs_7_, ...), custom_call_target="tpu_custom_call", output_to_operand_aliasing={{}: (3, {})} | custom-call | flops 37748736 | bytes 2400000 | tf_op jit(solution)/shard_map/attend/pallas_call | solution.py:619
  112.0 7.0 %collective-permute-done.20.refs_1_ = bf16[48,16,2,256]{3,2,1,0:T(2,128)(2,1)S(1)} collective-permute-done((bf16[48,16,2,256]{3,2,1,0:T(2,128)(2,1)S(1)}, bf16[48,16,2,256]{3,2,1,0:T(2,128)(2,1)S(1)}, u32[]{:S(2)}, u32[]{:S(2)}) %collective-permute-start.20) | collective-permute-done | bytes 786464 | tf_op jit(solution)/shard_map/ppermute | solution.py:705
  119.0 3.2 %step.20 = (bf16[16,48,16,2,256]{4,3,2,1,0:T(2,128)(2,1)}, bf16[768,16,2,256]{3,2,1,0:T(2,128)(2,1)}, bf16[16,16,128]{2,1,0:T(8,128)(2,1)}, bf16[48,16,2,256]{3,...) custom-call(s32[1153]{0:T(1024)S(1)} %concatenate.7.table.refs_0_, ...), custom_call_target="tpu_custom_call", output_to_operand_aliasing={{0}: (6, {}), {1}: (7, {}), {2}: (8, {})} | custom-call | bytes 6000000 | tf_op jit(solution)/shard_map/step/pallas_call | solution.py:439
  127.2 8.7 %collective-permute-done.18.refs_1_ = bf16[48,16,2,256]{3,2,1,0:T(2,128)(2,1)S(1)} collective-permute-done((bf16[48,16,2,256]{3,2,1,0:T(2,128)(2,1)S(1)}, bf16[48,16,2,256]{3,2,1,0:T(2,128)(2,1)S(1)}, u32[]{:S(2)}, u32[]{:S(2)}) %collective-permute-start.18) | collective-permute-done | bytes 786464 | tf_op jit(solution)/shard_map/ppermute | solution.py:705
  141.4 3.9 %attend.18.refs_6_ = bf16[16,16,128]{2,1,0:T(8,128)(2,1)} custom-call(s32[1153]{0:T(1024)S(1)} %concatenate.7.table.refs_0_, bf16[16,3,16,128]{3,2,1,0:T(8,128)(2,1)} %pad_maximum_fusion.refs_1_.refs_4_.refs_5_.refs_3_, bf16[768,16,2,256]{3,2,1,0:T(2,128)(2,1)} %get-tuple-element.201.refs_2_.refs_5_, ...), custom_call_target="tpu_custom_call", output_to_operand_aliasing={{}: (3, {})} | custom-call | flops 37748736 | bytes 2400000 | tf_op jit(solution)/shard_map/attend/pallas_call | solution.py:619
  145.3 3.2 %step.23 = (bf16[16,48,16,2,256]{4,3,2,1,0:T(2,128)(2,1)}, bf16[768,16,2,256]{3,2,1,0:T(2,128)(2,1)}, bf16[16,16,128]{2,1,0:T(8,128)(2,1)}) custom-call(s32[1153]{0:T(1024)S(1)} %concatenate.7.table.refs_0_, bf16[48,16,2,256]{3,2,1,0:T(2,128)(2,1)} %collective-permute-done.26.refs_1_, ...), custom_call_target="tpu_custom_call", output_to_operand_aliasing={{0}: (4, {}), {1}: (5, {}), {2}: (6, {})} | custom-call | bytes 6000000 | tf_op jit(solution)/shard_map/step/pallas_call | solution.py:439
  148.4 2.5 %collective-permute-done.24.refs_1_ = bf16[48,16,2,256]{3,2,1,0:T(2,128)(2,1)S(1)} collective-permute-done((bf16[48,16,2,256]{3,2,1,0:T(2,128)(2,1)}, bf16[48,16,2,256]{3,2,1,0:T(2,128)(2,1)S(1)}, u32[]{:S(2)}, u32[]{:S(2)}) %collective-permute-start.24) | collective-permute-done | bytes 786464 | tf_op jit(solution)/shard_map/ppermute | solution.py:705
  150.9 3.5 %step.24 = (bf16[16,48,16,2,256]{4,3,2,1,0:T(2,128)(2,1)}, bf16[768,16,2,256]{3,2,1,0:T(2,128)(2,1)}, bf16[16,16,128]{2,1,0:T(8,128)(2,1)}) custom-call(s32[1153]{0:T(1024)S(1)} %concatenate.7.table.refs_0_, bf16[48,16,2,256]{3,2,1,0:T(2,128)(2,1)S(1)} %collective-permute-done.24.refs_1_, ...), custom_call_target="tpu_custom_call", output_to_operand_aliasing={{0}: (5, {}), {1}: (6, {}), {2}: (7, {})} | custom-call | bytes 6000000 | tf_op jit(solution)/shard_map/step/pallas_call | solution.py:439
  154.4 3.0 %collective-permute-done.23.refs_1_ = bf16[48,16,2,256]{3,2,1,0:T(2,128)(2,1)} collective-permute-done((bf16[48,16,2,256]{3,2,1,0:T(2,128)(2,1)}, bf16[48,16,2,256]{3,2,1,0:T(2,128)(2,1)}, u32[]{:S(2)}, u32[]{:S(2)}) %collective-permute-start.23) | collective-permute-done | bytes 786464 | tf_op jit(solution)/shard_map/ppermute | solution.py:705
  (81 shorter events, 32.4 us)
Async XLA Ops:
  0.6 25.3 %copy-start = (bf16[5120,256]{1,0:T(8,128)(2,1)S(1)}, bf16[5120,256]{1,0:T(8,128)(2,1)}, u32[]{:S(2)}) copy-start(bf16[5120,256]{1,0:T(8,128)(2,1)} %param.14) | copy-start | bytes 7864324
  0.6 15.3 %copy-start.4 = (s32[128,48]{0,1:T(8,128)S(1)}, s32[128,48]{0,1:T(8,128)}, u32[]{:S(2)}) copy-start(s32[128,48]{0,1:T(8,128)} %param.19) | copy-start | bytes 73732
  0.7 10.9 %copy-start.2 = (s32[128]{0:T(128)S(1)}, s32[128]{0:T(128)}, u32[]{:S(2)}) copy-start(s32[128]{0:T(128)} %param.20) | copy-start | bytes 1540
  0.7 11.0 %copy-start.3 = (s32[128]{0:T(128)S(1)}, s32[128]{0:T(128)}, u32[]{:S(2)}) copy-start(s32[128]{0:T(128)} %param.21) | copy-start | bytes 1540
  1.8 18.6 %copy-start.5 = (bf16[16,1280]{1,0:T(8,128)(2,1)S(1)}, bf16[16,1280]{1,0:T(8,128)(2,1)}, u32[]{:S(2)}) copy-start(bf16[16,1280]{1,0:T(8,128)(2,1)} %param.12) | copy-start | bytes 122884
  6.9 38.3 %collective-permute-start.6 = (bf16[96,16,2,256]{3,2,1,0:T(2,128)(2,1)}, bf16[96,16,2,256]{3,2,1,0:T(2,128)(2,1)}, u32[]{:S(2)}, u32[]{:S(2)}) collective-permute-start(bf16[96,16,2,256]{3,2,1,0:T(2,128)(2,1)} %get-tuple-element.144.token), channel_id=1, source_target_pairs={{0,8},{1,9},{2,10},{3,11},{4,12},{5,13},{6,14},{7,15},{8,0},{9,1},... | collective-permute-start | bytes 4718600 | tf_op jit(solution)/shard_map/ppermute | solution.py:705
  10.5 34.7 %collective-permute-start.7 = (bf16[96,16,2,256]{3,2,1,0:T(2,128)(2,1)}, bf16[96,16,2,256]{3,2,1,0:T(2,128)(2,1)}, u32[]{:S(2)}, u32[]{:S(2)}) collective-permute-start(bf16[96,16,2,256]{3,2,1,0:T(2,128)(2,1)} %get-tuple-element.145), channel_id=1, source_target_pairs={{0,1},{1,0},{2,3},{3,2},{4,5},{5,4},{6,7},{7,6},{8,16},{9,17},{10,... | collective-permute-start | bytes 4718600 | tf_op jit(solution)/shard_map/ppermute | solution.py:705
  10.5 40.5 %collective-permute-start.10 = (bf16[96,16,2,256]{3,2,1,0:T(2,128)(2,1)}, bf16[96,16,2,256]{3,2,1,0:T(2,128)(2,1)}, u32[]{:S(2)}, u32[]{:S(2)}) collective-permute-start(bf16[96,16,2,256]{3,2,1,0:T(2,128)(2,1)} %get-tuple-element.150), channel_id=1, source_target_pairs={{0,4},{1,5},{2,6},{3,7},{4,0},{5,1},{6,2},{7,3},{8,12},{9,13},{10,... | collective-permute-start | bytes 4718600 | tf_op jit(solution)/shard_map/ppermute | solution.py:705
  28.6 8.8 %copy-start.6 = (f32[128]{0:T(128)S(1)}, f32[128]{0:T(128)}, u32[]{:S(2)}) copy-start(f32[128]{0:T(128)} %param.17) | copy-start | bytes 1540
  28.6 8.9 %copy-start.7 = (f32[128]{0:T(128)S(1)}, f32[128]{0:T(128)}, u32[]{:S(2)}) copy-start(f32[128]{0:T(128)} %param.16) | copy-start | bytes 1540
  47.5 21.0 %collective-permute-start.8 = (bf16[48,16,2,256]{3,2,1,0:T(2,128)(2,1)S(1)}, bf16[48,16,2,256]{3,2,1,0:T(2,128)(2,1)S(1)}, u32[]{:S(2)}, u32[]{:S(2)}) collective-permute-start(bf16[48,16,2,256]{3,2,1,0:T(2,128)(2,1)S(1)} %get-tuple-element.148), channel_id=1, source_target_pairs={{0,8},{1,9},{2,10},{3,11},{4,12},{5,13},{6,14},{7,15},{8,0},{9,1},... | collective-permute-start | bytes 2359304 | tf_op jit(solution)/shard_map/ppermute | solution.py:705
  50.0 18.5 %collective-permute-start.9 = (bf16[48,16,2,256]{3,2,1,0:T(2,128)(2,1)S(1)}, bf16[48,16,2,256]{3,2,1,0:T(2,128)(2,1)S(1)}, u32[]{:S(2)}, u32[]{:S(2)}) collective-permute-start(bf16[48,16,2,256]{3,2,1,0:T(2,128)(2,1)S(1)} %get-tuple-element.149), channel_id=1, source_target_pairs={{0,1},{1,0},{2,3},{3,2},{4,5},{5,4},{6,7},{7,6},{8,16},{9,17},{10,... | collective-permute-start | bytes 2359304 | tf_op jit(solution)/shard_map/ppermute | solution.py:705
  50.0 20.2 %collective-permute-start.11 = (bf16[48,16,2,256]{3,2,1,0:T(2,128)(2,1)S(1)}, bf16[48,16,2,256]{3,2,1,0:T(2,128)(2,1)S(1)}, u32[]{:S(2)}, u32[]{:S(2)}) collective-permute-start(bf16[48,16,2,256]{3,2,1,0:T(2,128)(2,1)S(1)} %get-tuple-element.159), channel_id=1, source_target_pairs={{0,4},{1,5},{2,6},{3,7},{4,0},{5,1},{6,2},{7,3},{8,12},{9,13},{10,... | collective-permute-start | bytes 2359304 | tf_op jit(solution)/shard_map/ppermute | solution.py:705
  55.8 29.4 %collective-permute-start.14 = (bf16[48,16,2,256]{3,2,1,0:T(2,128)(2,1)S(1)}, bf16[48,16,2,256]{3,2,1,0:T(2,128)(2,1)S(1)}, u32[]{:S(2)}, u32[]{:S(2)}) collective-permute-start(bf16[48,16,2,256]{3,2,1,0:T(2,128)(2,1)S(1)} %get-tuple-element.162), channel_id=1, source_target_pairs={{0,8},{1,9},{2,10},{3,11},{4,12},{5,13},{6,14},{7,15},{8,0},{9,1},... | collective-permute-start | bytes 2359304 | tf_op jit(solution)/shard_map/ppermute | solution.py:705
  58.3 27.0 %collective-permute-start.15 = (bf16[48,16,2,256]{3,2,1,0:T(2,128)(2,1)S(1)}, bf16[48,16,2,256]{3,2,1,0:T(2,128)(2,1)S(1)}, u32[]{:S(2)}, u32[]{:S(2)}) collective-permute-start(bf16[48,16,2,256]{3,2,1,0:T(2,128)(2,1)S(1)} %get-tuple-element.163), channel_id=1, source_target_pairs={{0,1},{1,0},{2,3},{3,2},{4,5},{5,4},{6,7},{7,6},{8,16},{9,17},{10,... | collective-permute-start | bytes 2359304 | tf_op jit(solution)/shard_map/ppermute | solution.py:705
  70.2 22.7 %collective-permute-start.16 = (bf16[48,16,2,256]{3,2,1,0:T(2,128)(2,1)S(1)}, bf16[48,16,2,256]{3,2,1,0:T(2,128)(2,1)S(1)}, u32[]{:S(2)}, u32[]{:S(2)}) collective-permute-start(bf16[48,16,2,256]{3,2,1,0:T(2,128)(2,1)S(1)} %get-tuple-element.170), channel_id=1, source_target_pairs={{0,4},{1,5},{2,6},{3,7},{4,0},{5,1},{6,2},{7,3},{8,12},{9,13},{10,... | collective-permute-start | bytes 2359304 | tf_op jit(solution)/shard_map/ppermute | solution.py:705
  72.5 29.7 %collective-permute-start.12 = (bf16[48,16,2,256]{3,2,1,0:T(2,128)(2,1)S(1)}, bf16[48,16,2,256]{3,2,1,0:T(2,128)(2,1)S(1)}, u32[]{:S(2)}, u32[]{:S(2)}) collective-permute-start(bf16[48,16,2,256]{3,2,1,0:T(2,128)(2,1)S(1)} %get-tuple-element.160), channel_id=1, source_target_pairs={{0,8},{1,9},{2,10},{3,11},{4,12},{5,13},{6,14},{7,15},{8,0},{9,1},... | collective-permute-start | bytes 2359304 | tf_op jit(solution)/shard_map/ppermute | solution.py:705
  74.4 27.7 %collective-permute-start.13 = (bf16[48,16,2,256]{3,2,1,0:T(2,128)(2,1)S(1)}, bf16[48,16,2,256]{3,2,1,0:T(2,128)(2,1)S(1)}, u32[]{:S(2)}, u32[]{:S(2)}) collective-permute-start(bf16[48,16,2,256]{3,2,1,0:T(2,128)(2,1)S(1)} %get-tuple-element.161), channel_id=1, source_target_pairs={{0,1},{1,0},{2,3},{3,2},{4,5},{5,4},{6,7},{7,6},{8,16},{9,17},{10,... | collective-permute-start | bytes 2359304 | tf_op jit(solution)/shard_map/ppermute | solution.py:705
  87.6 20.5 %collective-permute-start.17 = (bf16[48,16,2,256]{3,2,1,0:T(2,128)(2,1)S(1)}, bf16[48,16,2,256]{3,2,1,0:T(2,128)(2,1)S(1)}, u32[]{:S(2)}, u32[]{:S(2)}) collective-permute-start(bf16[48,16,2,256]{3,2,1,0:T(2,128)(2,1)S(1)} %get-tuple-element.177), channel_id=1, source_target_pairs={{0,4},{1,5},{2,6},{3,7},{4,0},{5,1},{6,2},{7,3},{8,12},{9,13},{10,... | collective-permute-start | bytes 2359304 | tf_op jit(solution)/shard_map/ppermute | solution.py:705
  92.9 26.1 %collective-permute-start.20 = (bf16[48,16,2,256]{3,2,1,0:T(2,128)(2,1)S(1)}, bf16[48,16,2,256]{3,2,1,0:T(2,128)(2,1)S(1)}, u32[]{:S(2)}, u32[]{:S(2)}) collective-permute-start(bf16[48,16,2,256]{3,2,1,0:T(2,128)(2,1)S(1)} %get-tuple-element.180), channel_id=1, source_target_pairs={{0,8},{1,9},{2,10},{3,11},{4,12},{5,13},{6,14},{7,15},{8,0},{9,1},... | collective-permute-start | bytes 2359304 | tf_op jit(solution)/shard_map/ppermute | solution.py:705
  95.3 23.7 %collective-permute-start.21 = (bf16[48,16,2,256]{3,2,1,0:T(2,128)(2,1)S(1)}, bf16[48,16,2,256]{3,2,1,0:T(2,128)(2,1)S(1)}, u32[]{:S(2)}, u32[]{:S(2)}) collective-permute-start(bf16[48,16,2,256]{3,2,1,0:T(2,128)(2,1)S(1)} %get-tuple-element.181), channel_id=1, source_target_pairs={{0,1},{1,0},{2,3},{3,2},{4,5},{5,4},{6,7},{7,6},{8,16},{9,17},{10,... | collective-permute-start | bytes 2359304 | tf_op jit(solution)/shard_map/ppermute | solution.py:705
  104.4 18.4 %collective-permute-start.22 = (bf16[48,16,2,256]{3,2,1,0:T(2,128)(2,1)S(1)}, bf16[48,16,2,256]{3,2,1,0:T(2,128)(2,1)S(1)}, u32[]{:S(2)}, u32[]{:S(2)}) collective-permute-start(bf16[48,16,2,256]{3,2,1,0:T(2,128)(2,1)S(1)} %get-tuple-element.188), channel_id=1, source_target_pairs={{0,4},{1,5},{2,6},{3,7},{4,0},{5,1},{6,2},{7,3},{8,12},{9,13},{10,... | collective-permute-start | bytes 2359304 | tf_op jit(solution)/shard_map/ppermute | solution.py:705
  108.1 27.7 %collective-permute-start.18 = (bf16[48,16,2,256]{3,2,1,0:T(2,128)(2,1)S(1)}, bf16[48,16,2,256]{3,2,1,0:T(2,128)(2,1)S(1)}, u32[]{:S(2)}, u32[]{:S(2)}) collective-permute-start(bf16[48,16,2,256]{3,2,1,0:T(2,128)(2,1)S(1)} %get-tuple-element.178), channel_id=1, source_target_pairs={{0,8},{1,9},{2,10},{3,11},{4,12},{5,13},{6,14},{7,15},{8,0},{9,1},... | collective-permute-start | bytes 2359304 | tf_op jit(solution)/shard_map/ppermute | solution.py:705
  108.1 27.7 %collective-permute-start.19 = (bf16[48,16,2,256]{3,2,1,0:T(2,128)(2,1)S(1)}, bf16[48,16,2,256]{3,2,1,0:T(2,128)(2,1)S(1)}, u32[]{:S(2)}, u32[]{:S(2)}) collective-permute-start(bf16[48,16,2,256]{3,2,1,0:T(2,128)(2,1)S(1)} %get-tuple-element.179), channel_id=1, source_target_pairs={{0,1},{1,0},{2,3},{3,2},{4,5},{5,4},{6,7},{7,6},{8,16},{9,17},{10,... | collective-permute-start | bytes 2359304 | tf_op jit(solution)/shard_map/ppermute | solution.py:705
  122.8 22.4 %collective-permute-start.26 = (bf16[48,16,2,256]{3,2,1,0:T(2,128)(2,1)}, bf16[48,16,2,256]{3,2,1,0:T(2,128)(2,1)}, u32[]{:S(2)}, u32[]{:S(2)}) collective-permute-start(bf16[48,16,2,256]{3,2,1,0:T(2,128)(2,1)} %get-tuple-element.196), channel_id=1, source_target_pairs={{0,4},{1,5},{2,6},{3,7},{4,0},{5,1},{6,2},{7,3},{8,12},{9,13},{10,... | collective-permute-start | bytes 2359304 | tf_op jit(solution)/shard_map/ppermute | solution.py:705
  124.4 26.5 %collective-permute-start.24 = (bf16[48,16,2,256]{3,2,1,0:T(2,128)(2,1)}, bf16[48,16,2,256]{3,2,1,0:T(2,128)(2,1)S(1)}, u32[]{:S(2)}, u32[]{:S(2)}) collective-permute-start(bf16[48,16,2,256]{3,2,1,0:T(2,128)(2,1)} %get-tuple-element.194), channel_id=1, source_target_pairs={{0,8},{1,9},{2,10},{3,11},{4,12},{5,13},{6,14},{7,15},{8,0},{9,1},... | collective-permute-start | bytes 2359304 | tf_op jit(solution)/shard_map/ppermute | solution.py:705
  127.1 23.8 %collective-permute-start.25 = (bf16[48,16,2,256]{3,2,1,0:T(2,128)(2,1)}, bf16[48,16,2,256]{3,2,1,0:T(2,128)(2,1)}, u32[]{:S(2)}, u32[]{:S(2)}) collective-permute-start(bf16[48,16,2,256]{3,2,1,0:T(2,128)(2,1)} %get-tuple-element.195), channel_id=1, source_target_pairs={{0,1},{1,0},{2,3},{3,2},{4,5},{5,4},{6,7},{7,6},{8,16},{9,17},{10,... | collective-permute-start | bytes 2359304 | tf_op jit(solution)/shard_map/ppermute | solution.py:705
  137.5 19.9 %collective-permute-start.23 = (bf16[48,16,2,256]{3,2,1,0:T(2,128)(2,1)}, bf16[48,16,2,256]{3,2,1,0:T(2,128)(2,1)}, u32[]{:S(2)}, u32[]{:S(2)}) collective-permute-start(bf16[48,16,2,256]{3,2,1,0:T(2,128)(2,1)} %get-tuple-element.193), channel_id=1, source_target_pairs={{0,4},{1,5},{2,6},{3,7},{4,0},{5,1},{6,2},{7,3},{8,12},{9,13},{10,... | collective-permute-start | bytes 2359304 | tf_op jit(solution)/shard_map/ppermute | solution.py:705
  159.2 1.8 %copy-start.1 = (bf16[5120,256]{1,0:T(8,128)(2,1)S(1)}, bf16[5120,256]{1,0:T(8,128)(2,1)}, u32[]{:S(2)}) copy-start(bf16[5120,256]{1,0:T(8,128)(2,1)} %param.14) | copy-start | bytes 7864324
